TPU v7x, 256 devices: a whole 4x4x8 slice. The times are simulated.
256 devices in a mesh: dp: 8 (over z), expert: 32 (over y, x, core).
Axes of the slice: x: 4, y: 4, z: 8, core: 2. Of those that a mesh axis runs over, the one named last changes fastest.
Arguments:
- queries: bfloat16 [512, 32, 576], P(('dp', 'expert')), may hold values from -32 to 32
- new_latent: bfloat16 [512, 576], P(('dp', 'expert')), may hold values from -4 to 4
- pool_pages: bfloat16 [1536, 576, 128], P(('dp', 'expert')), may hold values from -4 to 4
- page_owner: int32 [8, 32, 2, 8], P(None, 'expert'), may hold values from 0 to 7, as said below
- page_slot: int32 [8, 32, 2, 8], P(None, 'expert'), may hold values from 0 to 5
- lengths: int32 [512], P(('dp', 'expert')), may hold values from 128 to 1024, as said below
- residual: bfloat16 [512, 7168], P('dp', 'expert'), may hold values from -20 to 20
- value_weight: bfloat16 [32, 512, 128], replicated, may hold values from -1 to 1
- output_weight: bfloat16 [4096, 7168], P(None, 'expert'), may hold values from -0.09375 to 0.09375
- norm_gain: float32 [7168], P('expert'), may hold values from 0.25 to 1.75
- expert_ids: int32 [512, 8], P('dp'), may hold values from 0 to 31, all different within a row; in each aligned block of 64 rows (0 to 63, 64 to 127, ...) at most 24 rows name the same one
- route_gates: float32 [512, 8], P('dp'), may hold values from 0.05 to 0.4
- expert_in: bfloat16 [32, 7168, 2, 1024], P('dp', 'expert'), may hold values from -0.0625 to 0.0625
- expert_out: bfloat16 [32, 1024, 7168], P('dp', None, 'expert'), may hold values from -0.1875 to 0.1875
Outputs:
- mixed: bfloat16 [512, 7168], P('dp', 'expert')
Inputs may be any that keep to these rules, and one draw needn't show every extreme that they name: `expert_ids`: in each aligned block of 64 rows (the rows of one index of dp) a row names 8 different experts and no expert is named by more than 24 rows. `page_owner`: among the 16 page entries of the rows of one device, no index of dp is named more than 3 times, and in every such set one index is named exactly 3 times. `lengths`: in every attention group some row has exactly 1024 tokens and some row exactly 128.
All inputs are finite; a program needn't handle non-finite values.
Results may differ from a plain program's by a relative error of at most 0.0075.
Values may be sent and summed in bfloat16 or wider, within the bound.
A program may use at most 128 MiB of HBM per device.

v0:
```python
import jax
import jax.numpy as jnp
from jax import lax
from jax.sharding import PartitionSpec as P

D = 7168
KVR = 512
ROPE = 64
DV = 128
TOP = 8


epsilon = 1e-06


def route_tables(expert_ids, experts, capacity):
    group_rows, chosen = expert_ids.shape
    flattened = expert_ids.reshape(-1)
    matches = (flattened[:, None] == jnp.arange(experts, dtype=jnp.int32)[None, :]).astype(
        jnp.int32
    )
    earlier = jnp.sum((jnp.cumsum(matches, axis=0) - matches) * matches, axis=1)
    target_index = flattened * capacity + earlier
    source_rows = jnp.arange(group_rows * chosen, dtype=jnp.int32) // chosen
    source_table = (
        jnp.full((experts * capacity,), group_rows, jnp.int32).at[target_index].set(source_rows)
    )
    return (target_index.reshape(group_rows, chosen), source_table)


def body(
    queries,
    new_latent,
    pool_pages,
    page_owner,
    page_slot,
    lengths,
    residual,
    value_weight,
    output_weight,
    norm_gain,
    expert_ids,
    route_gates,
    expert_in,
    expert_out,
):
    groups = lax.axis_size("dp")
    my_group = lax.axis_index("dp")
    row_count, head_count, latent_width = queries.shape
    page_count = page_owner.shape[3]
    page_tokens = pool_pages.shape[2]
    requests = row_count * page_count
    page_capacity = (3 * requests + 2 * groups - 1) // (2 * groups)
    owners = page_owner[:, 0].reshape(groups, requests)
    local_slots = page_slot[:, 0].reshape(groups, requests)
    matches = (owners[:, :, None] == jnp.arange(groups, dtype=jnp.int32)[None, None, :]).astype(
        jnp.int32
    )
    earlier = jnp.sum((jnp.cumsum(matches, axis=1) - matches) * matches, axis=2)
    requester = jnp.arange(groups, dtype=jnp.int32)[:, None]
    target_index = jnp.where(
        owners == my_group, requester * page_capacity + earlier, groups * page_capacity
    )
    send_table = (
        jnp.zeros((groups * page_capacity + 1,), jnp.int32)
        .at[target_index.reshape(-1)]
        .set(local_slots.reshape(-1))
    )
    outgoing = pool_pages[send_table[:-1]].reshape(groups, page_capacity, latent_width, page_tokens)
    incoming = lax.all_to_all(outgoing, "dp", split_axis=0, concat_axis=0, tiled=True)
    my_owners = lax.dynamic_index_in_dim(owners, my_group, 0, keepdims=False)
    my_earlier = lax.dynamic_index_in_dim(earlier, my_group, 0, keepdims=False)
    flat_pages = incoming.reshape(groups * page_capacity, latent_width, page_tokens)
    page_keys = flat_pages[my_owners * page_capacity + my_earlier].reshape(
        row_count, page_count, latent_width, page_tokens
    )
    score_scale = (DV + ROPE) ** (-0.5)
    scores = (
        jnp.einsum("rhc,rpct->rhpt", queries, page_keys, preferred_element_type=jnp.float32)
        * score_scale
    )
    self_score = (
        jnp.einsum("rhc,rc->rh", queries, new_latent, preferred_element_type=jnp.float32)
        * score_scale
    )
    position = (
        jnp.arange(page_count, dtype=jnp.int32)[:, None] * page_tokens
        + jnp.arange(page_tokens, dtype=jnp.int32)[None, :]
    )
    valid = position[None] < lengths[:, None, None]
    scores = jnp.where(valid[:, None], scores, -jnp.inf)
    highest = jnp.maximum(jnp.max(scores, axis=(2, 3)), self_score)
    expo = jnp.exp(scores - highest[:, :, None, None])
    self_expo = jnp.exp(self_score - highest)
    denominator = jnp.sum(expo, axis=(2, 3)) + self_expo
    weights = (expo / denominator[:, :, None, None]).astype(jnp.bfloat16)
    self_weight = (self_expo / denominator).astype(jnp.bfloat16)
    summed = jnp.einsum("rhpt,rpct->rhc", weights, page_keys, preferred_element_type=jnp.float32)
    summed = (
        summed
        + self_weight.astype(jnp.float32)[:, :, None] * new_latent.astype(jnp.float32)[:, None, :]
    )
    latent_out = summed[:, :, :KVR].astype(jnp.bfloat16)
    head_values = jnp.einsum(
        "rhc,hcv->rhv", latent_out, value_weight, preferred_element_type=jnp.float32
    )
    head_values = head_values.astype(jnp.bfloat16).reshape(row_count, head_count * DV)
    projected = jnp.dot(
        lax.all_gather(head_values, "expert", axis=0, tiled=True),
        output_weight,
        preferred_element_type=jnp.float32,
    )
    resid = (residual.astype(jnp.float32) + projected).astype(jnp.bfloat16)
    group_rows, width_share = resid.shape
    local_experts = expert_in.shape[0]
    experts = local_experts * groups
    capacity = min(group_rows, (3 * group_rows * TOP + 2 * experts - 1) // (2 * experts))
    route_index, source_table = route_tables(expert_ids, experts, capacity)
    padded = jnp.concatenate([resid, jnp.zeros((1, width_share), jnp.bfloat16)], axis=0)
    outgoing_rows = padded[source_table].reshape(groups, local_experts, capacity, width_share)
    values_wide = lax.all_to_all(
        outgoing_rows, "dp", split_axis=0, concat_axis=0, tiled=True
    ).astype(jnp.float32)
    squares = jnp.sum(values_wide * values_wide, axis=3)
    scaled = (values_wide * norm_gain).astype(jnp.bfloat16)
    gate_up = jnp.einsum("secd,edkf->seckf", scaled, expert_in, preferred_element_type=jnp.float32)
    gate_total, square_total = lax.psum((gate_up, squares), "expert")
    inverse = lax.rsqrt(square_total / D + epsilon)
    gate_total = gate_total * inverse[..., None, None]
    hidden = (jax.nn.silu(gate_total[:, :, :, 0]) * gate_total[:, :, :, 1]).astype(jnp.bfloat16)
    result = jnp.einsum("secf,efd->secd", hidden, expert_out, preferred_element_type=jnp.float32)
    returned = lax.all_to_all(
        result.astype(jnp.bfloat16), "dp", split_axis=0, concat_axis=0, tiled=True
    )
    flat_back = returned.reshape(experts * capacity, width_share)
    picked = flat_back[route_index]
    combined = jnp.einsum("gt,gtd->gd", route_gates, picked.astype(jnp.float32))
    return (resid.astype(jnp.float32) + combined).astype(jnp.bfloat16)


def solution(mesh):
    in_specs = (
        P(("dp", "expert"), None, None),
        P(("dp", "expert"), None),
        P(("dp", "expert"), None, None),
        P(None, "expert", None, None),
        P(None, "expert", None, None),
        P(("dp", "expert")),
        P("dp", "expert"),
        P(),
        P(None, "expert"),
        P("expert"),
        P("dp", None),
        P("dp", None),
        P("dp", "expert", None, None),
        P("dp", None, "expert"),
    )
    out_specs = P("dp", "expert")
    return jax.shard_map(body, mesh=mesh, in_specs=in_specs, out_specs=out_specs, check_vma=False)
```

profile of v0, /device:TPU:1, one launch (start us, length us, event | category | flops | bytes accessed | tf_op | source)
XLA Modules:
  0.0 324.9 jit_solution(12827135841455642967)
XLA Ops:
  6.5 0.0 copy-start
  6.5 0.9 copy.93
  7.4 0.4 fusion.58
  7.9 0.7 broadcast_compare_fusion
  8.6 0.1 eq.59
  8.7 0.1 copy.68
  8.7 0.1 broadcast_add_fusion
  8.8 0.1 add.152
  8.9 0.8 reshape.225
  9.7 1.0 scatter_custom_fusion
  10.7 4.1 %gather_fusion = bf16[24,576,128]{2,1,0:T(8,128)(2,1)} fusion(bf16[6,576,128]{2,1,0:T(8,128)(2,1)} %param.16, s32[1024]{0:T(1024)S(1)} %pad_clamp_fusion.3), kind=kCustom, calls=%fused_computation | custom fusion | bytes 7077984 | tf_op jit(solution)/shard_map/gather | solution.py:69
  14.8 9.2 %all-to-all-start = ((bf16[8,3,576,128]{3,2,1,0:T(8,128)(2,1)}), bf16[8,3,576,128]{3,2,1,0:T(8,128)(2,1)}, u32[]{:S(2)}, u32[]{:S(2)}) async-start(bf16[8,3,576,128]{3,2,1,0:T(8,128)(2,1)} %bitcast.108), calls=%async_computation | async-start | bytes 7077888 | tf_op jit(solution)/shard_map/all_to_all | solution.py:70
  24.0 0.0 all-reduce.3.cloned.1.call-start
  24.0 0.0 copy-done.5
  24.0 0.1 copy.71
  24.1 0.1 eq.68
  24.2 0.1 eq.64
  24.3 0.0 copy-done.4
  24.3 1.2 reduce-window.6
  25.5 0.2 slice_reduce_fusion
  25.8 0.1 fusion.38
  25.9 0.1 reduce_sum.45
  26.0 0.1 mul.115
  26.1 2.4 scatter_custom_fusion.1
  28.6 0.2 add_reduce_fusion
  28.8 0.1 iota_add_fusion
  28.9 0.0 copy-done.8
  28.9 0.1 broadcast_compare_fusion.1
  29.0 0.0 copy-done.2
  29.0 0.1 fusion.44
  29.1 77.7 %all-to-all-done = bf16[8,3,576,128]{3,2,1,0:T(8,128)(2,1)} async-done(((bf16[8,3,576,128]{3,2,1,0:T(8,128)(2,1)}), bf16[8,3,576,128]{3,2,1,0:T(8,128)(2,1)}, u32[]{:S(2)}, u32[]{:S(2)}) %all-to-all-start) | async-done | bytes 3538976 | tf_op jit(solution)/shard_map/all_to_all | solution.py:70
  106.8 4.3 %gather_fusion.1 = bf16[16,576,128]{2,1,0:T(8,128)(2,1)} fusion(bf16[24,576,128]{2,1,0:T(8,128)(2,1)} %bitcast.2, s32[1024]{0:T(1024)S(1)} %pad_clamp_fusion.2), kind=kCustom, calls=%fused_computation.1 | custom fusion | bytes 4718656 | tf_op jit(solution)/shard_map/gather | solution.py:74
  111.1 2.4 fusion.59
  113.5 0.2 fusion.31
  113.7 0.0 copy-done.1
  113.7 0.8 convolution_bitcast_fusion
  114.5 0.1 fusion.32
  114.6 2.8 fusion.24
  117.4 25.4 %all-gather = bf16[32,2,4096]{2,1,0:T(2,128)(2,1)S(1)} all-gather(bf16[1,2,4096]{2,1,0:T(2,128)(2,1)S(1)} %fusion.24), channel_id=1, replica_groups=mesh['dp'=8,'expert'=32] {'expert'}, dimensions={0}, use_global_device_ids=true | all-gather | bytes 540672 | tf_op jit(solution)/shard_map/all_gather | solution.py:109
  142.8 0.2 reshape.242
  143.1 0.0 copy-done.3
  143.1 0.0 copy-start.7
  143.1 2.2 fusion.23
  145.3 2.7 gather_fusion.2
  148.0 17.6 %all_to_all.15 = bf16[8,4,24,224]{3,2,1,0:T(8,128)(2,1)S(1)} all-to-all(bf16[8,4,24,224]{3,2,1,0:T(8,128)(2,1)S(1)} %bitcast.110), channel_id=1, replica_groups=mesh['dp'=8,'expert'=32] {'dp'}, dimensions={0} | all-to-all | bytes 688128 | tf_op jit(solution)/shard_map/all_to_all | solution.py:121
  165.5 0.0 copy-done.7
  165.5 0.2 fusion.26
  165.7 6.3 %fusion.4 = f32[8,4,24,2,1024]{4,2,3,0,1:T(8,128)} fusion(bf16[4,224,2,1024,1]{3,2,1,0,4:T(2,128)(2,1)} %bitcast.109, bf16[8,4,24,224,1]{3,2,1,0,4:T(8,128)(2,1)S(1)} %get-tuple-element.6), kind=kOutput, calls=%fused_computation.13 | convolution fusion | flops 704643072 | bytes 10305536 | tf_op jit(solution)/shard_map/secd,edkf->seckf/dot_general | solution.py:126
  172.1 0.0 all-reduce.3.cloned.1.call-update
  172.1 121.8 %psum.15 = f32[8,4,24]{2,0,1:T(8,128)S(1)} all-reduce(f32[8,4,24]{2,0,1:T(8,128)S(1)} %copy.77), channel_id=1, replica_groups=mesh['dp'=8,'expert'=32] {'expert'}, use_global_device_ids=true, to_apply=%region_11.12 | all-reduce | flops 768 | bytes 6144 | tf_op jit(solution)/shard_map/psum | solution.py:127
  293.9 0.0 all-reduce.3.cloned.1.call-done
  293.9 3.3 %broadcast_multiply_fusion = f32[8,4,24,2,1024]{4,2,3,0,1:T(8,128)S(1)} fusion(f32[8,4,24,2,1024]{4,2,3,0,1:T(8,128)} %all-reduce.3.cloned.1.call-done, f32[8,4,24]{2,0,1:T(8,128)S(1)} %add_rsqrt_fusion), kind=kLoop, calls=%fused_computation.12 | loop fusion | flops 1572864 | bytes 12585984 | tf_op jit(solution)/shard_map/mul | solution.py:129
  297.2 0.0 copy-done
  297.2 0.0 copy-start.6
  297.2 1.3 fusion.15
  298.5 0.8 copy.79
  299.2 5.2 %all-to-all-start.2 = ((bf16[8,4,24,224]{3,2,1,0:T(8,128)(2,1)}), bf16[8,4,24,224]{3,2,1,0:T(8,128)(2,1)S(1)}, u32[]{:S(2)}, u32[]{:S(2)}) async-start(bf16[8,4,24,224]{3,2,1,0:T(8,128)(2,1)} %copy.79), calls=%async_computation.2 | async-start | bytes 786432 | tf_op jit(solution)/shard_map/all_to_all | solution.py:132
  304.4 0.1 reshape.215
  304.5 0.0 copy-done.6
  304.5 0.1 copy.87
  304.6 10.6 %all-to-all-done.2 = bf16[8,4,24,224]{3,2,1,0:T(8,128)(2,1)S(1)} async-done(((bf16[8,4,24,224]{3,2,1,0:T(8,128)(2,1)}), bf16[8,4,24,224]{3,2,1,0:T(8,128)(2,1)S(1)}, u32[]{:S(2)}, u32[]{:S(2)}) %all-to-all-start.2) | async-done | bytes 344096 | tf_op jit(solution)/shard_map/all_to_all | solution.py:132
  315.2 1.9 gather_fusion.3
  317.2 0.2 fusion.29
  317.4 0.6 fusion.39
  (28 shorter events, 0.2 us)
Async XLA Ops:
  6.5 290.6 %copy-start = (bf16[4,1024,224]{1,2,0:T(8,128)(2,1)S(1)}, bf16[4,1024,224]{1,2,0:T(8,128)(2,1)}, u32[]{:S(2)}) copy-start(bf16[4,1024,224]{1,2,0:T(8,128)(2,1)} %param.27) | copy-start | bytes 5505028
  14.8 9.2 %copy-start.5 = (s32[64,8]{0,1:T(8,128)S(1)}, s32[64,8]{0,1:T(8,128)}, u32[]{:S(2)}) copy-start(s32[64,8]{0,1:T(8,128)} %param.24) | copy-start | bytes 6148
  14.8 9.5 %copy-start.4 = (bf16[2,576]{1,0:T(2,128)(2,1)S(1)}, bf16[2,576]{1,0:T(2,128)(2,1)}, u32[]{:S(2)}) copy-start(bf16[2,576]{1,0:T(2,128)(2,1)} %param.15) | copy-start | bytes 6916
  14.8 14.1 %copy-start.8 = (s32[2]{0:T(128)S(1)}, s32[2]{0:T(128)}, u32[]{:S(2)}) copy-start(s32[2]{0:T(128)} %param.19) | copy-start | bytes 28
  14.8 14.1 %copy-start.2 = (bf16[2,32,576]{2,1,0:T(8,128)(2,1)S(1)}, bf16[2,32,576]{2,1,0:T(8,128)(2,1)}, u32[]{:S(2)}) copy-start(bf16[2,32,576]{2,1,0:T(8,128)(2,1)} %param.14) | copy-start | bytes 221188
  14.8 92.0 %all-to-all-start = ((bf16[8,3,576,128]{3,2,1,0:T(8,128)(2,1)}), bf16[8,3,576,128]{3,2,1,0:T(8,128)(2,1)}, u32[]{:S(2)}, u32[]{:S(2)}) async-start(bf16[8,3,576,128]{3,2,1,0:T(8,128)(2,1)} %bitcast.108), calls=%async_computation | async-start | bytes 7077888 | tf_op jit(solution)/shard_map/all_to_all | solution.py:70
  24.0 269.9 %all-reduce.3.cloned.1.call-start = ((), (), s32[]{:S(2)}) async-start(), calls=%async_computation.3 | async-start | bytes 12582912 | tf_op jit(solution)/shard_map/psum | solution.py:127
  111.1 2.6 copy-start.1
  114.5 28.6 %copy-start.3 = (bf16[64,224]{1,0:T(8,128)(2,1)S(1)}, bf16[64,224]{1,0:T(8,128)(2,1)}, u32[]{:S(2)}) copy-start(bf16[64,224]{1,0:T(8,128)(2,1)} %param.20) | copy-start | bytes 86020
  143.1 22.5 %copy-start.7 = (f32[224]{0:T(256)S(1)}, f32[224]{0:T(256)}, u32[]{:S(2)}) copy-start(f32[224]{0:T(256)} %param.23) | copy-start | bytes 2692
  297.2 7.3 %copy-start.6 = (f32[64,8]{0,1:T(8,128)S(1)}, f32[64,8]{0,1:T(8,128)}, u32[]{:S(2)}) copy-start(f32[64,8]{0,1:T(8,128)} %param.25) | copy-start | bytes 6148
  299.2 16.0 %all-to-all-start.2 = ((bf16[8,4,24,224]{3,2,1,0:T(8,128)(2,1)}), bf16[8,4,24,224]{3,2,1,0:T(8,128)(2,1)S(1)}, u32[]{:S(2)}, u32[]{:S(2)}) async-start(bf16[8,4,24,224]{3,2,1,0:T(8,128)(2,1)} %copy.79), calls=%async_computation.2 | async-start | bytes 786432 | tf_op jit(solution)/shard_map/all_to_all | solution.py:132
Sparse Core Ops, SparseCore 0:
  172.2 120.1 all-reduce.2
where the time goes:
time: 329 us; the launch traced here: 325 us
  blocking collectives  165 us (50%)
  waiting for transfers between devices  88.3 us (27%)
  local copies, waits for them, and re-layouts  20.2 us (6%)
  matrix products  16.2 us (5%)
  starting transfers between devices  14.4 us (4%)
  between operations  13.7 us (4%)
  other arithmetic  7.35 us (2%)
    psum x1, blocking collectives, body(): gate_total, square_total = lax.psum((gate_up, squares), 'expert')  122 us
    all_to_all x1, waiting for transfers between devices, body(): lax.all_to_all(outgoing, 'dp', split_axis=0, concat_axis=0, tiled=True)  77.7 us
    all_gather x1, blocking collectives, body(): lax.all_gather(head_values, 'expert', axis=0, tiled=True)  25.4 us
    all_to_all x1, blocking collectives, body(): lax.all_to_all(outgoing_rows, 'dp', split_axis=0, concat_axis=0, tiled=True)  17.6 us
    all_to_all x1, waiting for transfers between devices, body(): lax.all_to_all(result.astype(jnp.bfloat16), 'dp', split_axis=0, concat_ax...  10.6 us
    all_to_all x1, starting transfers between devices, body(): lax.all_to_all(outgoing, 'dp', split_axis=0, concat_axis=0, tiled=True)  9.16 us
  transfers between devices with their start and end apart: 3, of which 2 were waited for; matrix products, arithmetic and copies ran while one was open for 2% of the time, Pallas kernels for 0%

commit v1 on v0

v1 whole, which is shorter than its diff:
```python
import functools
import jax
import jax.numpy as jnp
from jax import lax
from jax.experimental import pallas as pl
from jax.experimental.pallas import tpu as pltpu
from jax.sharding import PartitionSpec as P

D = 7168
KVR = 512
ROPE = 64
DV = 128
TOP = 8
EPS = 1e-06
MESH = pl.DeviceIdType.MESH
F32 = jnp.float32
BF16 = jnp.bfloat16
NEG = -1e30


def iota(shape, dim):
    return lax.broadcasted_iota(jnp.int32, shape, dim)


def mm(a, b):
    return jnp.dot(a, b, preferred_element_type=F32)


def mm_nt(a, b):
    return lax.dot_general(a, b, (((1,), (1,)), ((), ())), preferred_element_type=F32)


def kernel(
    G, C, ELOC, CAPX,
    q_hbm, nl_ref, pool_hbm, owner_ref, slot_ref, len_ref, res_ref, wv_hbm, wo_hbm, gain_ref,
    ids_ref, gates_ref, win_hbm, wout_hbm,
    out_ref,
    kc, vt, nlp, q_all, sml_s, sml_r, perm, perm_t, o_all, o_hm, hv_hm, hv_s, lse_s, hv_r, lse_r,
    hva, xmat, wv, wo, win, wg, wout, xall, xsib, sq_s, sq_r, inv_s, inv_r,
    sel, sel_t, gcol, part, prs, hid, vown, vsib, zsib_s, zsib_r, zs, zr, zown,
    lsem, s_q, r_q, s_sml, r_sml, s_hv, r_hv, s_lse, r_lse, s_x, r_x, s_inv, r_inv, s_z, r_z,
    s_hva, r_hva, s_sq, r_sq, s_prs, r_prs, s_hid, r_hid, s_fw, r_fw, s_w, r_w,
):
    g = lax.axis_index("dp")
    k = lax.axis_index("expert")
    core = lax.rem(k, 2)
    chip = lax.div(k, 2)
    sib = k + 1 - 2 * core
    NC = C // 2
    ROWS, H, LAT = q_all.shape[1:]
    NS = pool_hbm.shape[0]
    PAGE = pool_hbm.shape[2]
    RH = ROWS * H
    GROUP = C * ROWS
    W = res_ref.shape[1]
    FF = win_hbm.shape[3]
    FH = FF // 2
    ESL = G * CAPX
    RCH = ELOC * ESL // NC
    CPE = NC // ELOC
    NR = G * ROWS

    def dp_peer(d):
        half = lax.div(d + 1, 2)
        off = half * (2 * lax.rem(d, 2) - 1)
        return lax.rem(g + off + G, G)

    def ex_peer(d):
        return lax.rem(k + d, C)

    def chip_peer(d):
        return lax.rem(chip + d, NC)

    def rcopy(src, dst, ss, rs, dev):
        return pltpu.make_async_remote_copy(
            src_ref=src, dst_ref=dst, send_sem=ss, recv_sem=rs, device_id=dev, device_id_type=MESH
        )

    def loop(lo, hi, fn):
        lax.fori_loop(lo, hi, lambda i, c: (fn(i), c)[1], 0)

    def exp_dev(kk):
        return (g, kk)

    def dp_dev(j):
        return (j, k)

    locals_ = []
    for s in range(NS):
        locals_.append(
            pltpu.make_async_copy(pool_hbm.at[s], kc.at[:, pl.ds(s * PAGE, PAGE)], lsem.at[s])
        )
    c_q = pltpu.make_async_copy(q_hbm, q_all.at[g], lsem.at[NS])
    c_win = pltpu.make_async_copy(
        win_hbm.at[:, :, :, pl.ds(pl.multiple_of(core * FH, FH), FH)], win.at[0], lsem.at[NS + 1]
    )
    c_wv = pltpu.make_async_copy(wv_hbm, wv, lsem.at[NS + 2])
    c_wo = pltpu.make_async_copy(wo_hbm, wo, lsem.at[NS + 3])
    c_wout = pltpu.make_async_copy(
        wout_hbm.at[:, :, pl.ds(pl.multiple_of(core * FH, FH), FH)], wout.at[0], lsem.at[NS + 4]
    )
    c_q.start()
    for c in locals_:
        c.start()
    for c in (c_win, c_wv, c_wo, c_wout):
        c.start()

    barrier = pltpu.get_barrier_semaphore()

    def sig_dp(d):
        pl.semaphore_signal(barrier, inc=1, device_id=dp_dev(lax.rem(g + d, G)), device_id_type=MESH)

    def sig_ex(d):
        pl.semaphore_signal(barrier, inc=1, device_id=exp_dev(ex_peer(d)), device_id_type=MESH)

    loop(1, G, sig_dp)
    loop(1, C, sig_ex)

    ids = ids_ref[...]
    gates = gates_ref[...]
    e_iota = iota((G * ELOC, GROUP), 0)
    named = jnp.zeros((G * ELOC, GROUP), F32)
    gval = jnp.zeros((G * ELOC, GROUP), F32)
    for t in range(TOP):
        hit = ids[t : t + 1, :] == e_iota
        named = named + hit.astype(F32)
        gval = gval + jnp.where(hit, gates[t : t + 1, :], 0.0)
    tri = (iota((GROUP, GROUP), 0) < iota((GROUP, GROUP), 1)).astype(BF16)
    rank = mm(named.astype(BF16), tri)
    code = jnp.where(named > 0, rank, -1.0)
    lane = iota((8, 128), 0)
    lens = jnp.where(lane == 0, len_ref[0], len_ref[1]).astype(F32)
    sml_s[...] = jnp.zeros_like(sml_s)
    for j in range(G):
        sml_s[j, 0:ELOC, 0:GROUP] = code[j * ELOC : (j + 1) * ELOC]
        sml_s[j, ELOC : 2 * ELOC, 0:GROUP] = gval[j * ELOC : (j + 1) * ELOC]
        sml_s[j, 8:16, :] = lens
    sml_r[g] = sml_s[g]

    c_q.wait()
    pl.semaphore_wait(barrier, G - 1 + C - 1)

    def send_q(d):
        j = dp_peer(d)
        rcopy(sml_s.at[j], sml_r.at[g], s_sml.at[j], r_sml.at[g], dp_dev(j)).start()
        rcopy(q_all.at[g], q_all.at[g], s_q.at[j], r_q.at[g], dp_dev(j)).start()

    loop(1, G, send_q)

    other = pl.multiple_of((1 - core) * FH, FH)
    w1 = rcopy(win_hbm.at[:, :, :, pl.ds(other, FH)], win.at[1], s_w.at[0], r_w.at[0], exp_dev(sib))
    w2 = rcopy(wout_hbm.at[:, :, pl.ds(other, FH)], wout.at[1], s_w.at[1], r_w.at[1], exp_dev(sib))
    w1.start()
    w2.start()

    N2 = NR * H
    pr = iota((N2, 1), 0)
    perm[...] = (iota((N2, N2), 1) == lax.rem(pr, NR) * H + lax.div(pr, NR)).astype(BF16)
    perm_t[...] = (iota((N2, N2), 1) == lax.rem(pr, H) * NR + lax.div(pr, H)).astype(BF16)
    nl = nl_ref[...].astype(F32)
    nrow = iota((128, LAT), 0)
    nacc = jnp.zeros((128, LAT), F32)
    for s in range(ROWS):
        nacc = jnp.where(nrow == s, nl[s : s + 1, :], nacc)
    nlp[...] = nacc.astype(BF16)
    for c in locals_:
        c.wait()
    vt[...] = kc[0:KVR, :].T

    scale = (DV + ROPE) ** (-0.5)
    NT = NS * PAGE

    def attend(src, own):
        q = q_all[src].reshape(RH, LAT)
        sc = mm(q, kc[...]) * scale
        lid = iota((1, NT), 1)
        slot_lane = lax.div(lid, PAGE)
        tpos = lax.rem(lid, PAGE).astype(F32)
        rows = []
        lv = sml_r[src, 8:16, :]
        for s in range(ROWS):
            ln = lv[s : s + 1, 0:1]
            cnt = jnp.zeros((1, NT), F32)
            for p in range(owner_ref.shape[3]):
                here = jnp.where(owner_ref[src, 0, s, p] == g, slot_ref[src, 0, s, p], -1)
                ok = jnp.logical_and(slot_lane == here, tpos + float(p * PAGE) < ln)
                cnt = cnt + ok.astype(F32)
            rows.append(jnp.broadcast_to(cnt, (H, NT)))
        cnt = jnp.concatenate(rows, axis=0)
        scm = jnp.where(cnt > 0, sc, NEG)
        top = jnp.max(scm, axis=1, keepdims=True)
        if own:
            cs = (iota((RH, 128), 1) == lax.div(iota((RH, 128), 0), H)).astype(F32)
            ss = jnp.where(cs > 0, mm_nt(q, nlp[...]) * scale, NEG)
            top = jnp.maximum(top, jnp.max(ss, axis=1, keepdims=True))
        p = cnt * jnp.exp(scm - top)
        den = jnp.sum(p, axis=1, keepdims=True)
        acc = mm(p.astype(BF16), vt[...])
        if own:
            pself = cs * jnp.exp(ss - top)
            den = den + jnp.sum(pself, axis=1, keepdims=True)
            acc = acc + mm(pself.astype(BF16), nlp[:, 0:KVR])
        has = den > 0
        inv_den = jnp.where(has, 1.0 / jnp.where(has, den, 1.0), 0.0)
        lse = jnp.where(has, top + jnp.log(jnp.where(has, den, 1.0)), NEG)
        o_all[pl.ds(pl.multiple_of(src * RH, RH), RH), :] = (acc * inv_den).astype(BF16)
        row = jnp.broadcast_to(lse, (RH, 128)).T[0:8]
        lse_s[src] = jnp.concatenate([row, row], axis=1)

    attend(g, True)

    c_win.wait()
    rcopy(win.at[1], win.at[1], s_w.at[0], r_w.at[0], exp_dev(sib)).wait_recv()
    col = iota((W, 2 * W), 1)
    two = 2 * iota((W, 2 * W), 0)
    pick_g = (col == two).astype(BF16)
    pick_u = (col == two + 1).astype(BF16)

    def split(i):
        e = lax.div(i, 2)
        o = lax.rem(i, 2)
        w = win[o, e].reshape(2 * W, FH)
        wg[e, o, :, 0:FH] = mm(pick_g, w).astype(BF16)
        wg[e, o, :, FH : 2 * FH] = mm(pick_u, w).astype(BF16)

    loop(0, 2 * ELOC, split)

    def chunk(d):
        src = dp_peer(d)
        rcopy(sml_r.at[src], sml_r.at[src], s_sml.at[src], r_sml.at[src], dp_dev(src)).wait_recv()
        rcopy(q_all.at[src], q_all.at[src], s_q.at[src], r_q.at[src], dp_dev(src)).wait_recv()
        attend(src, False)

    loop(1, G, chunk)

    o_hm[...] = mm(perm[...], o_all[...]).astype(BF16)
    c_wv.wait()
    HB = 8

    def project(b):
        for i in range(HB):
            h = b * HB + i
            at = pl.ds(pl.multiple_of(h * NR, NR), NR)
            hv_hm[at, :] = mm(o_hm[at, :], wv[h]).astype(BF16)

    loop(0, H // HB, project)
    hv_s[...] = mm(perm_t[...], hv_hm[...]).astype(BF16).reshape(G, RH, DV)
    hv_r[g] = hv_s[g]
    lse_r[g] = lse_s[g]

    def send_hv(d):
        j = dp_peer(d)
        rcopy(lse_s.at[j], lse_r.at[g], s_lse.at[j], r_lse.at[g], dp_dev(j)).start()
        rcopy(hv_s.at[j], hv_r.at[g], s_hv.at[j], r_hv.at[g], dp_dev(j)).start()

    loop(1, G, send_hv)

    siota = iota((ESL, G * GROUP), 0).astype(F32)
    for e in range(ELOC):
        codes = []
        gvals = []
        for j in range(G):
            cj = sml_r[j, e : e + 1, 0:GROUP]
            codes.append(jnp.where(cj >= 0, cj + float(j * CAPX), -1.0))
            gvals.append(sml_r[j, ELOC + e : ELOC + e + 1, 0:GROUP])
        crow = jnp.concatenate(codes, axis=1)
        grow = jnp.concatenate(gvals, axis=1)
        hit = siota == crow
        sel[e] = hit.astype(F32).astype(BF16)
        gs = jnp.sum(jnp.where(hit, grow, 0.0), axis=1, keepdims=True)
        gcol[e] = jnp.broadcast_to(gs, (ESL, 128))
    sel_t[...] = sel[...].reshape(ELOC * ESL, G * GROUP).T

    def wait_hv(d):
        j = dp_peer(d)
        rcopy(lse_r.at[j], lse_r.at[j], s_lse.at[j], r_lse.at[j], dp_dev(j)).wait_recv()
        rcopy(hv_r.at[j], hv_r.at[j], s_hv.at[j], r_hv.at[j], dp_dev(j)).wait_recv()

    loop(1, G, wait_hv)
    riota = iota((8, 128), 0)
    ls = jnp.full((8, 128), NEG, F32)
    for j in range(G):
        ls = jnp.where(riota == j, lse_r[j], ls)
    wts = jnp.exp(ls - jnp.max(ls, axis=0, keepdims=True))
    wts = wts / jnp.sum(wts, axis=0, keepdims=True)
    wcol = wts.T
    comb = jnp.zeros((RH, DV), F32)
    for j in range(G):
        comb = comb + wcol[0:RH, j : j + 1] * hv_r[j].astype(F32)
    hva[k] = comb.astype(BF16)

    def send_hva(d):
        j = ex_peer(d)
        rcopy(hva.at[k], hva.at[k], s_hva.at[j], r_hva.at[k], exp_dev(j)).start()

    loop(1, C, send_hva)
    c_wo.wait()

    def wait_hva(d):
        j = ex_peer(d)
        rcopy(hva.at[j], hva.at[j], s_hva.at[j], r_hva.at[j], exp_dev(j)).wait_recv()

    loop(1, C, wait_hva)

    for b in range(C // G):
        blk = mm(perm[...], hva[b * G : (b + 1) * G].reshape(N2, DV)).astype(BF16)
        for h in range(H):
            xmat[b * NR : (b + 1) * NR, h * DV : (h + 1) * DV] = blk[h * NR : (h + 1) * NR]
    proj = mm_nt(xmat[...], wo[...])
    resid = (res_ref[...].astype(F32) + proj).astype(BF16).astype(F32)
    xall[g] = (resid * gain_ref[...].reshape(1, W)).astype(BF16)

    def send_x(d):
        j = dp_peer(d)
        rcopy(xall.at[g], xall.at[g], s_x.at[j], r_x.at[g], dp_dev(j)).start()

    def fwd(j):
        rcopy(xall.at[j], xsib.at[j], s_fw.at[j], r_fw.at[j], exp_dev(sib)).start()

    loop(1, G, send_x)
    fwd(g)
    sq = jnp.sum(resid * resid, axis=1, keepdims=True)
    sq_row = jnp.broadcast_to(sq, (GROUP, 128)).T[0:8]
    sq_s[...] = jnp.concatenate([sq_row] * (128 // GROUP), axis=1)
    sq_r[k] = sq_s[...]

    def send_sq(d):
        j = ex_peer(d)
        rcopy(sq_s, sq_r.at[k], s_sq.at[j], r_sq.at[k], exp_dev(j)).start()

    loop(1, C, send_sq)

    def pass_x(d):
        j = dp_peer(d)
        rcopy(xall.at[j], xall.at[j], s_x.at[j], r_x.at[j], dp_dev(j)).wait_recv()
        fwd(j)

    loop(1, G, pass_x)

    def wait_fw(j):
        rcopy(xsib.at[j], xsib.at[j], s_fw.at[j], r_fw.at[j], exp_dev(sib)).wait_recv()

    loop(0, G, wait_fw)

    e0 = lax.div(chip, CPE)

    def part_step(i):
        e = lax.rem(e0 + i, ELOC)
        xo = mm(sel[e], xall[...].reshape(G * GROUP, W)).astype(BF16)
        xs = mm(sel[e], xsib[...].reshape(G * GROUP, W)).astype(BF16)
        at = pl.ds(pl.multiple_of(e * ESL, 16), ESL)
        for f in range(2):
            cols = slice(f * FH, (f + 1) * FH)
            part[at, cols] = (mm(xo, wg[e, 0, :, cols]) + mm(xs, wg[e, 1, :, cols])).astype(BF16)

        def send(t):
            c = e * CPE + lax.rem(chip + t, CPE)

            @pl.when(c != chip)
            def _():
                rcopy(
                    part.at[pl.ds(pl.multiple_of(c * RCH, 16), RCH)], prs.at[chip],
                    s_prs.at[c], r_prs.at[chip], exp_dev(2 * c + core),
                ).start()

        loop(0, CPE, send)

    loop(0, ELOC, part_step)
    mine = pl.ds(pl.multiple_of(chip * RCH, 16), RCH)
    prs[chip] = part[mine, :]

    def wait_sq(d):
        j = ex_peer(d)
        rcopy(sq_r.at[j], sq_r.at[j], s_sq.at[j], r_sq.at[j], exp_dev(j)).wait_recv()

    loop(1, C, wait_sq)
    inv_s[...] = lax.rsqrt(jnp.sum(sq_r[...], axis=0) / D + EPS)
    inv_r[g] = inv_s[...]

    def send_inv(d):
        j = dp_peer(d)
        rcopy(inv_s, inv_r.at[g], s_inv.at[j], r_inv.at[g], dp_dev(j)).start()

    loop(1, G, send_inv)

    def wait_inv(d):
        j = dp_peer(d)
        rcopy(inv_r.at[j], inv_r.at[j], s_inv.at[j], r_inv.at[j], dp_dev(j)).wait_recv()

    loop(1, G, wait_inv)
    irow = jnp.concatenate([inv_r[j, 0:1, 0:GROUP] for j in range(G)], axis=1)
    my_sel = sel[lax.div(chip, CPE), pl.ds(pl.multiple_of(lax.rem(chip, CPE) * RCH, 16), RCH), :]
    icol = jnp.sum(my_sel.astype(F32) * irow, axis=1, keepdims=True)

    def wait_prs(d):
        c = chip_peer(d)
        rcopy(prs.at[c], prs.at[c], s_prs.at[c], r_prs.at[c], exp_dev(2 * c + core)).wait_recv()

    loop(1, NC, wait_prs)
    tot = prs[0].astype(F32)
    for c in range(1, NC):
        tot = tot + prs[c].astype(F32)
    tot = tot * icol
    ga = tot[:, 0:FH]
    hid[mine, :] = (ga / (1.0 + jnp.exp(-ga)) * tot[:, FH : 2 * FH]).astype(BF16)

    def send_hid(d):
        c = chip_peer(d)
        rcopy(hid.at[mine], hid.at[mine], s_hid.at[c], r_hid.at[chip], exp_dev(2 * c + core)).start()

    loop(1, NC, send_hid)
    c_wout.wait()
    rcopy(wout.at[1], wout.at[1], s_w.at[1], r_w.at[1], exp_dev(sib)).wait_recv()

    def wait_hid(d):
        c = chip_peer(d)
        at = pl.ds(pl.multiple_of(c * RCH, 16), RCH)
        rcopy(hid.at[at], hid.at[at], s_hid.at[c], r_hid.at[c], exp_dev(2 * c + core)).wait_recv()

    loop(1, NC, wait_hid)

    def down(e):
        at = pl.ds(pl.multiple_of(e * ESL, 16), ESL)
        he = hid[at, :]
        gs = gcol[e, :, 0:1]
        vsib[at, :] = (mm_nt(he, wout[1, e]) * gs).astype(BF16)
        vown[at, :] = (mm_nt(he, wout[0, e]) * gs).astype(BF16)

    loop(0, ELOC, down)
    zsib_s[...] = mm(sel_t[...], vsib[...]).astype(BF16)
    zc = rcopy(zsib_s, zsib_r, s_w.at[2], r_w.at[2], exp_dev(sib))
    zc.start()
    zown[...] = mm(sel_t[...], vown[...])
    zc.wait_recv()
    zsum = zown[...] + zsib_r[...].astype(F32)
    zown[...] = zsum
    zs[...] = zsum.astype(BF16).reshape(G, GROUP, W)

    def send_z(d):
        j = dp_peer(d)
        rcopy(zs.at[j], zr.at[g], s_z.at[j], r_z.at[g], dp_dev(j)).start()

    loop(1, G, send_z)
    zr[g] = jnp.zeros((GROUP, W), BF16)
    total = resid + zown[pl.ds(pl.multiple_of(g * GROUP, GROUP), GROUP), :]

    def wait_z(d):
        j = dp_peer(d)
        rcopy(zr.at[j], zr.at[j], s_z.at[j], r_z.at[j], dp_dev(j)).wait_recv()

    loop(1, G, wait_z)
    for j in range(G):
        total = total + zr[j].astype(F32)
    out_ref[...] = total.astype(BF16)

    w1.wait_send()
    w2.wait_send()
    zc.wait_send()

    def drain_dp(d):
        j = dp_peer(d)
        dev = dp_dev(j)
        rcopy(sml_s.at[j], sml_r.at[g], s_sml.at[j], r_sml.at[g], dev).wait_send()
        rcopy(q_all.at[g], q_all.at[g], s_q.at[j], r_q.at[g], dev).wait_send()
        rcopy(lse_s.at[j], lse_r.at[g], s_lse.at[j], r_lse.at[g], dev).wait_send()
        rcopy(hv_s.at[j], hv_r.at[g], s_hv.at[j], r_hv.at[g], dev).wait_send()
        rcopy(xall.at[g], xall.at[g], s_x.at[j], r_x.at[g], dev).wait_send()
        rcopy(inv_s, inv_r.at[g], s_inv.at[j], r_inv.at[g], dev).wait_send()
        rcopy(zs.at[j], zr.at[g], s_z.at[j], r_z.at[g], dev).wait_send()

    loop(1, G, drain_dp)

    def drain_ex(d):
        j = ex_peer(d)
        dev = exp_dev(j)
        rcopy(hva.at[k], hva.at[k], s_hva.at[j], r_hva.at[k], dev).wait_send()
        rcopy(sq_s, sq_r.at[k], s_sq.at[j], r_sq.at[k], dev).wait_send()

    loop(1, C, drain_ex)

    def drain_fw(j):
        rcopy(xall.at[j], xsib.at[j], s_fw.at[j], r_fw.at[j], exp_dev(sib)).wait_send()

    loop(0, G, drain_fw)

    def drain_ch(d):
        c = chip_peer(d)
        dev = exp_dev(2 * c + core)
        at = pl.ds(pl.multiple_of(c * RCH, 16), RCH)
        rcopy(part.at[at], prs.at[chip], s_prs.at[c], r_prs.at[chip], dev).wait_send()
        rcopy(hid.at[mine], hid.at[mine], s_hid.at[c], r_hid.at[chip], dev).wait_send()

    loop(1, NC, drain_ch)


def body(
    queries, new_latent, pool_pages, page_owner, page_slot, lengths, residual, value_weight,
    output_weight, norm_gain, expert_ids, route_gates, expert_in, expert_out,
):
    G = lax.axis_size("dp")
    C = lax.axis_size("expert")
    ROWS, H, LAT = queries.shape
    NS, _, PAGE = pool_pages.shape
    GROUP, W = residual.shape
    ELOC, _, _, FF = expert_in.shape
    FH = FF // 2
    NC = C // 2
    RH = ROWS * H
    capacity = min(GROUP, (3 * GROUP * TOP + 2 * G * ELOC - 1) // (2 * G * ELOC))
    ESL = G * capacity
    SLOTS = ELOC * ESL
    RCH = SLOTS // NC
    N2 = G * RH
    ROWN = G * GROUP

    def v(shape, dtype=BF16):
        return pltpu.VMEM(shape, dtype)

    dma = lambda n: pltpu.SemaphoreType.DMA((n,))
    scratch = [
        v((LAT, NS * PAGE)), v((NS * PAGE, KVR)), v((128, LAT)), v((G, ROWS, H, LAT)),
        v((G, 16, 128), F32), v((G, 16, 128), F32), v((N2, N2)), v((N2, N2)),
        v((N2, KVR)), v((N2, KVR)), v((N2, DV)), v((G, RH, DV)), v((G, 8, 128), F32),
        v((G, RH, DV)), v((G, 8, 128), F32),
        v((C, RH, DV)), v((GROUP, H * DV)), v((H, KVR, DV)), v((W, H * DV)),
        v((2, ELOC, W, 2, FH)), v((ELOC, 2, W, FF)), v((2, ELOC, W, FH)),
        v((G, GROUP, W)), v((G, GROUP, W)), v((8, 128), F32), v((C, 8, 128), F32),
        v((8, 128), F32), v((G, 8, 128), F32),
        v((ELOC, ESL, ROWN)), v((ROWN, SLOTS)), v((ELOC, ESL, 128), F32),
        v((SLOTS, FF)), v((NC, RCH, FF)), v((SLOTS, FH)), v((SLOTS, W)), v((SLOTS, W)),
        v((ROWN, W)), v((ROWN, W)), v((G, GROUP, W)), v((G, GROUP, W)), v((ROWN, W), F32),
        dma(NS + 5),
    ]
    for n in (G, G, G, G, G, G, G, C, C, NC, NC, G, 3):
        scratch += [dma(n), dma(n)]
    vm = pl.BlockSpec(memory_space=pltpu.VMEM)
    sm = pl.BlockSpec(memory_space=pltpu.SMEM)
    hbm = pl.BlockSpec(memory_space=pl.ANY)
    return pl.pallas_call(
        functools.partial(kernel, G, C, ELOC, capacity),
        out_shape=jax.ShapeDtypeStruct((GROUP, W), BF16),
        in_specs=[hbm, vm, hbm, sm, sm, sm, vm, hbm, hbm, vm, vm, vm, hbm, hbm],
        out_specs=vm,
        scratch_shapes=scratch,
        compiler_params=pltpu.CompilerParams(
            collective_id=0, has_side_effects=True, vmem_limit_bytes=56 << 20
        ),
        cost_estimate=pl.CostEstimate(flops=4 << 30, bytes_accessed=16 << 20, transcendentals=1 << 20),
        name="decode_step",
    )(
        queries, new_latent, pool_pages, page_owner, page_slot, lengths, residual, value_weight,
        output_weight.T, norm_gain, expert_ids.T, route_gates.T, expert_in,
        jnp.swapaxes(expert_out, 1, 2),
    )


def solution(mesh):
    in_specs = (
        P(("dp", "expert"), None, None),
        P(("dp", "expert"), None),
        P(("dp", "expert"), None, None),
        P(None, "expert", None, None),
        P(None, "expert", None, None),
        P(("dp", "expert")),
        P("dp", "expert"),
        P(),
        P(None, "expert"),
        P("expert"),
        P("dp", None),
        P("dp", None),
        P("dp", "expert", None, None),
        P("dp", None, "expert"),
    )
    return jax.shard_map(
        body, mesh=mesh, in_specs=in_specs, out_specs=P("dp", "expert"), check_vma=False
    )
```

time: 329 us -> 114 us (0.35)
  blocking collectives: 165 us -> 0 us
  Pallas kernels: 0 us -> 112 us
  waiting for transfers between devices: 88.3 us -> 0 us
  local copies, waits for them, and re-layouts: 20.2 us -> 1.38 us
  matrix products: 16.2 us -> 0 us
  starting transfers between devices: 14.4 us -> 0 us
  between operations: 13.7 us -> 0.01 us
  other arithmetic: 7.35 us -> 0 us
    psum x1 -> x0, blocking collectives: 122 us -> none  [body(): gate_total, square_total = lax.psum((gate_up, squares), 'expert')]
    pallas_call x0 -> x1, Pallas kernels: none -> 112 us  [body(): pl.pallas_call(functools.partial(kernel, G, C, ELOC, capacity), out_shape...]
    all_to_all x2 -> x0, waiting for transfers between devices: 88.3 us -> none  [the longest x1 77.7 us: body(): lax.all_to_all(outgoing, 'dp', split_axis=0, concat_axis=0, tiled=True)]
    all_gather x1 -> x0, blocking collectives: 25.4 us -> none  [body(): lax.all_gather(head_values, 'expert', axis=0, tiled=True)]
    all_to_all x1 -> x0, blocking collectives: 17.6 us -> none  [body(): lax.all_to_all(outgoing_rows, 'dp', split_axis=0, concat_axis=0, tiled=True)]
    dot_general x8 -> x0, matrix products: 16.2 us -> none  [the longest x1 6.35 us: body(): jnp.einsum('secd,edkf->seckf', scaled, expert_in, preferred_element_type=...]
    all_to_all x2 -> x0, starting transfers between devices: 14.4 us -> none  [the longest x1 9.16 us: body(): lax.all_to_all(outgoing, 'dp', split_axis=0, concat_axis=0, tiled=True)]
    gather x4 -> x0, local copies, waits for them, and re-layouts: 13 us -> none  [the longest x1 4.28 us: body(): flat_pages[my_owners * page_capacity + my_earlier]]
  transfers between devices with their start and end apart: 3 -> 0, of which waited for: 2 -> 0; matrix products, arithmetic and copies ran while one was open for 2% -> 0% of each run, Pallas kernels for 0% -> 0%
where the time goes in v1:
time: 114 us; the launch traced here: 113 us
  Pallas kernels  112 us (98%)
  local copies, waits for them, and re-layouts  1.38 us (1%)
    pallas_call x1, Pallas kernels, body(): pl.pallas_call(functools.partial(kernel, G, C, ELOC, capacity), out_shape...  112 us

profile of v1, /device:TPU:1, one launch (start us, length us, event | category | flops | bytes accessed | tf_op | source)
XLA Modules:
  0.0 113.0 jit_solution(1083087533612076315)
XLA Ops:
  0.0 111.6 %decode_step.1 = bf16[64,224]{1,0:T(8,128)(2,1)} custom-call(bf16[2,32,576]{2,1,0:T(8,128)(2,1)} %q_hbm.1, bf16[2,576]{1,0:T(2,128)(2,1)} %nl_ref.1, bf16[6,576,128]{2,1,0:T(8,128)(2,1)} %pool_hbm.1, s32[8,1,2,8]{3,2,1,0:T(2,128)} %owner_ref.1, s32[8,1,2,8]{3,2,1,0:T(2,128)} %slot_ref.1, s32[2]{0:T(128)} %len_ref.1, bf16[64,224]{1,0:T(8,128)(2,1)} %res_ref.1, ...), custom_call_target="tpu_custom_call" | custom-call | flops 4294967296 | bytes 16777216 | tf_op jit(solution)/shard_map/decode_step/pallas_call | solution.py:539
  111.6 1.4 %copy.16 = bf16[64,224]{1,0:T(8,128)(2,1)} copy(bf16[64,224]{1,0:T(8,128)(2,1)} %decode_step.1) | data formatting | bytes 57344

commit v2 on v1

--- a/solution.py
+++ b/solution.py
@@ -35,19 +35,20 @@
     q_hbm, nl_ref, pool_hbm, owner_ref, slot_ref, len_ref, res_ref, wv_hbm, wo_hbm, gain_ref,
     ids_ref, gates_ref, win_hbm, wout_hbm,
     out_ref,
-    kc, vt, nlp, q_all, sml_s, sml_r, perm, perm_t, o_all, o_hm, hv_hm, hv_s, lse_s, hv_r, lse_r,
-    hva, xmat, wv, wo, win, wg, wout, xall, xsib, sq_s, sq_r, inv_s, inv_r,
-    sel, sel_t, gcol, part, prs, hid, vown, vsib, zsib_s, zsib_r, zs, zr, zown,
+    kc, vt, nlp, q_in, q_all, sml_s, sml_r, perm, perm_t, o_all, o_hm, hv_hm, hv_s, lse_s, hv_r,
+    lse_r, hva, xmat, wv, wo, win, wg, wout, xall, xsib, sq_s, sq_r, inv_s, inv_r,
+    sel, sel_t, gcol, part, in1, out1, b2, in2, hid, vown, vsib, zsib_s, zsib_r, zs, zr, zown,
     lsem, s_q, r_q, s_sml, r_sml, s_hv, r_hv, s_lse, r_lse, s_x, r_x, s_inv, r_inv, s_z, r_z,
-    s_hva, r_hva, s_sq, r_sq, s_prs, r_prs, s_hid, r_hid, s_fw, r_fw, s_w, r_w,
+    s_hva, r_hva, s_sq, r_sq, s_p1, r_p1, s_p2, r_p2, s_hid, r_hid, s_fw, r_fw, s_w, r_w,
 ):
     g = lax.axis_index("dp")
     k = lax.axis_index("expert")
     core = lax.rem(k, 2)
     chip = lax.div(k, 2)
     sib = k + 1 - 2 * core
-    NC = C // 2
-    ROWS, H, LAT = q_all.shape[1:]
+    cx = lax.rem(chip, 4)
+    cy = lax.div(chip, 4)
+    ROWS, H, LAT = q_in.shape
     NS = pool_hbm.shape[0]
     PAGE = pool_hbm.shape[2]
     RH = ROWS * H
@@ -56,20 +57,25 @@
     FF = win_hbm.shape[3]
     FH = FF // 2
     ESL = G * CAPX
-    RCH = ELOC * ESL // NC
-    CPE = NC // ELOC
+    QR = ESL // 4
+    QF = FH // 4
     NR = G * ROWS
 
     def dp_peer(d):
-        half = lax.div(d + 1, 2)
-        off = half * (2 * lax.rem(d, 2) - 1)
+        half = lax.div(G + 1 - d, 2)
+        off = half * (1 - 2 * lax.rem(G + 1 - d, 2))
+        return lax.rem(g + off + G, G)
+
+    def at_dp(off):
         return lax.rem(g + off + G, G)
 
     def ex_peer(d):
         return lax.rem(k + d, C)
 
-    def chip_peer(d):
-        return lax.rem(chip + d, NC)
+    def at_chip(ox, oy):
+        x = lax.rem(cx + ox + 4, 4)
+        y = lax.rem(cy + oy + 4, 4)
+        return x, y, (g, 2 * (4 * y + x) + core)
 
     def rcopy(src, dst, ss, rs, dev):
         return pltpu.make_async_remote_copy(
@@ -90,7 +96,7 @@
         locals_.append(
             pltpu.make_async_copy(pool_hbm.at[s], kc.at[:, pl.ds(s * PAGE, PAGE)], lsem.at[s])
         )
-    c_q = pltpu.make_async_copy(q_hbm, q_all.at[g], lsem.at[NS])
+    c_q = pltpu.make_async_copy(q_hbm, q_in, lsem.at[NS])
     c_win = pltpu.make_async_copy(
         win_hbm.at[:, :, :, pl.ds(pl.multiple_of(core * FH, FH), FH)], win.at[0], lsem.at[NS + 1]
     )
@@ -128,30 +134,11 @@
     tri = (iota((GROUP, GROUP), 0) < iota((GROUP, GROUP), 1)).astype(BF16)
     rank = mm(named.astype(BF16), tri)
     code = jnp.where(named > 0, rank, -1.0)
-    lane = iota((8, 128), 0)
-    lens = jnp.where(lane == 0, len_ref[0], len_ref[1]).astype(F32)
     sml_s[...] = jnp.zeros_like(sml_s)
     for j in range(G):
         sml_s[j, 0:ELOC, 0:GROUP] = code[j * ELOC : (j + 1) * ELOC]
         sml_s[j, ELOC : 2 * ELOC, 0:GROUP] = gval[j * ELOC : (j + 1) * ELOC]
-        sml_s[j, 8:16, :] = lens
     sml_r[g] = sml_s[g]
-
-    c_q.wait()
-    pl.semaphore_wait(barrier, G - 1 + C - 1)
-
-    def send_q(d):
-        j = dp_peer(d)
-        rcopy(sml_s.at[j], sml_r.at[g], s_sml.at[j], r_sml.at[g], dp_dev(j)).start()
-        rcopy(q_all.at[g], q_all.at[g], s_q.at[j], r_q.at[g], dp_dev(j)).start()
-
-    loop(1, G, send_q)
-
-    other = pl.multiple_of((1 - core) * FH, FH)
-    w1 = rcopy(win_hbm.at[:, :, :, pl.ds(other, FH)], win.at[1], s_w.at[0], r_w.at[0], exp_dev(sib))
-    w2 = rcopy(wout_hbm.at[:, :, pl.ds(other, FH)], wout.at[1], s_w.at[1], r_w.at[1], exp_dev(sib))
-    w1.start()
-    w2.start()
 
     N2 = NR * H
     pr = iota((N2, 1), 0)
@@ -163,6 +150,33 @@
     for s in range(ROWS):
         nacc = jnp.where(nrow == s, nl[s : s + 1, :], nacc)
     nlp[...] = nacc.astype(BF16)
+
+    c_q.wait()
+    for r in range(ROWS):
+        n = len_ref[r]
+        li = iota((H, q_all.shape[3] - LAT), 1)
+        tail = jnp.where(li == 0, lax.div(n, 32), jnp.where(li == 1, lax.rem(n, 32), 0))
+        q_all[g, r] = jnp.concatenate([q_in[r], tail.astype(F32).astype(BF16)], axis=1)
+    pl.semaphore_wait(barrier, G - 1 + C - 1)
+
+    def q_copy(i, src, off, row=None):
+        j = at_dp(off)
+        if row is None:
+            return rcopy(q_all.at[src], q_all.at[src], s_q.at[i], r_q.at[src], dp_dev(j))
+        return rcopy(
+            q_all.at[src, row], q_all.at[src, row], s_q.at[i], r_q.at[G + row], dp_dev(j)
+        )
+
+    q_sends = [q_copy(0, g, 2), q_copy(1, g, -2), q_copy(2, g, 1), q_copy(3, g, -1)]
+    for c in q_sends:
+        c.start()
+
+    other = pl.multiple_of((1 - core) * FH, FH)
+    w1 = rcopy(win_hbm.at[:, :, :, pl.ds(other, FH)], win.at[1], s_w.at[0], r_w.at[0], exp_dev(sib))
+    w2 = rcopy(wout_hbm.at[:, :, pl.ds(other, FH)], wout.at[1], s_w.at[1], r_w.at[1], exp_dev(sib))
+    w1.start()
+    w2.start()
+
     for c in locals_:
         c.wait()
     vt[...] = kc[0:KVR, :].T
@@ -171,15 +185,16 @@
     NT = NS * PAGE
 
     def attend(src, own):
-        q = q_all[src].reshape(RH, LAT)
+        qx = q_all[src].reshape(RH, q_all.shape[3])
+        q = qx[:, 0:LAT]
         sc = mm(q, kc[...]) * scale
         lid = iota((1, NT), 1)
         slot_lane = lax.div(lid, PAGE)
         tpos = lax.rem(lid, PAGE).astype(F32)
         rows = []
-        lv = sml_r[src, 8:16, :]
         for s in range(ROWS):
-            ln = lv[s : s + 1, 0:1]
+            lv = qx[s * H : s * H + 8, LAT : LAT + 2].astype(F32)
+            ln = lv[0:1, 0:1] * 32.0 + lv[0:1, 1:2]
             cnt = jnp.zeros((1, NT), F32)
             for p in range(owner_ref.shape[3]):
                 here = jnp.where(owner_ref[src, 0, s, p] == g, slot_ref[src, 0, s, p], -1)
@@ -204,34 +219,43 @@
         inv_den = jnp.where(has, 1.0 / jnp.where(has, den, 1.0), 0.0)
         lse = jnp.where(has, top + jnp.log(jnp.where(has, den, 1.0)), NEG)
         o_all[pl.ds(pl.multiple_of(src * RH, RH), RH), :] = (acc * inv_den).astype(BF16)
-        row = jnp.broadcast_to(lse, (RH, 128)).T[0:8]
+        row = jnp.broadcast_to(lse, (RH, 128)).T[0:1]
         lse_s[src] = jnp.concatenate([row, row], axis=1)
 
     attend(g, True)
 
-    c_win.wait()
-    rcopy(win.at[1], win.at[1], s_w.at[0], r_w.at[0], exp_dev(sib)).wait_recv()
-    col = iota((W, 2 * W), 1)
-    two = 2 * iota((W, 2 * W), 0)
-    pick_g = (col == two).astype(BF16)
-    pick_u = (col == two + 1).astype(BF16)
-
-    def split(i):
-        e = lax.div(i, 2)
-        o = lax.rem(i, 2)
-        w = win[o, e].reshape(2 * W, FH)
-        wg[e, o, :, 0:FH] = mm(pick_g, w).astype(BF16)
-        wg[e, o, :, FH : 2 * FH] = mm(pick_u, w).astype(BF16)
-
-    loop(0, 2 * ELOC, split)
+    for i, off in ((0, -2), (1, 2)):
+        src = at_dp(off)
+        q_copy(i, src, off).wait_recv()
+        for c in (q_copy(4 + i, src, 1 - 2 * i), q_copy(6 + i, src, 2 - 4 * i, row=i)):
+            c.start()
+            q_sends.append(c)
+
+    def send_sml(d):
+        j = dp_peer(d)
+        rcopy(sml_s.at[j], sml_r.at[g], s_sml.at[j], r_sml.at[g], dp_dev(j)).start()
+
+    loop(1, G, send_sml)
+
+    def ring(d):
+        n = lax.div(d, 2)
+        m = jnp.where(n == 0, 2, jnp.where(n == 1, 1, n + 1))
+        return at_dp(jnp.where(lax.rem(d, 2) == 0, -m, m))
+
+    def near(d):
+        attend(ring(d), False)
 
     def chunk(d):
-        src = dp_peer(d)
-        rcopy(sml_r.at[src], sml_r.at[src], s_sml.at[src], r_sml.at[src], dp_dev(src)).wait_recv()
-        rcopy(q_all.at[src], q_all.at[src], s_q.at[src], r_q.at[src], dp_dev(src)).wait_recv()
+        src = ring(d)
+        rcopy(q_all.at[src], q_all.at[src], s_q.at[0], r_q.at[src], dp_dev(src)).wait_recv()
         attend(src, False)
 
-    loop(1, G, chunk)
+    loop(0, 2, near)
+    loop(2, G - 2, chunk)
+    far = at_dp(G // 2)
+    for r in range(ROWS):
+        rcopy(q_all.at[far, r], q_all.at[far, r], s_q.at[0], r_q.at[G + r], dp_dev(far)).wait_recv()
+    attend(far, False)
 
     o_hm[...] = mm(perm[...], o_all[...]).astype(BF16)
     c_wv.wait()
@@ -255,6 +279,11 @@
 
     loop(1, G, send_hv)
 
+    def wait_sml(d):
+        j = dp_peer(d)
+        rcopy(sml_r.at[j], sml_r.at[j], s_sml.at[j], r_sml.at[j], dp_dev(j)).wait_recv()
+
+    loop(1, G, wait_sml)
     siota = iota((ESL, G * GROUP), 0).astype(F32)
     for e in range(ELOC):
         codes = []
@@ -294,6 +323,26 @@
         rcopy(hva.at[k], hva.at[k], s_hva.at[j], r_hva.at[k], exp_dev(j)).start()
 
     loop(1, C, send_hva)
+
+    c_win.wait()
+    rcopy(win.at[1], win.at[1], s_w.at[0], r_w.at[0], exp_dev(sib)).wait_recv()
+    col = iota((W, 2 * W), 1)
+    two = 2 * iota((W, 2 * W), 0)
+    pick_g = (col == two).astype(BF16)
+    pick_u = (col == two + 1).astype(BF16)
+
+    def split(i):
+        e = lax.div(i, 2)
+        o = lax.rem(i, 2)
+        w = win[o, e].reshape(2 * W, FH)
+        wgate = mm(pick_g, w).astype(BF16)
+        wup = mm(pick_u, w).astype(BF16)
+        for f in range(4):
+            wg[e, o, :, 2 * f * QF : (2 * f + 1) * QF] = wgate[:, f * QF : (f + 1) * QF]
+            wg[e, o, :, (2 * f + 1) * QF : 2 * (f + 1) * QF] = wup[:, f * QF : (f + 1) * QF]
+
+    loop(0, 2 * ELOC, split)
+
     c_wo.wait()
 
     def wait_hva(d):
@@ -320,7 +369,7 @@
     loop(1, G, send_x)
     fwd(g)
     sq = jnp.sum(resid * resid, axis=1, keepdims=True)
-    sq_row = jnp.broadcast_to(sq, (GROUP, 128)).T[0:8]
+    sq_row = jnp.broadcast_to(sq, (GROUP, 128)).T[0:1]
     sq_s[...] = jnp.concatenate([sq_row] * (128 // GROUP), axis=1)
     sq_r[k] = sq_s[...]
 
@@ -342,33 +391,6 @@
 
     loop(0, G, wait_fw)
 
-    e0 = lax.div(chip, CPE)
-
-    def part_step(i):
-        e = lax.rem(e0 + i, ELOC)
-        xo = mm(sel[e], xall[...].reshape(G * GROUP, W)).astype(BF16)
-        xs = mm(sel[e], xsib[...].reshape(G * GROUP, W)).astype(BF16)
-        at = pl.ds(pl.multiple_of(e * ESL, 16), ESL)
-        for f in range(2):
-            cols = slice(f * FH, (f + 1) * FH)
-            part[at, cols] = (mm(xo, wg[e, 0, :, cols]) + mm(xs, wg[e, 1, :, cols])).astype(BF16)
-
-        def send(t):
-            c = e * CPE + lax.rem(chip + t, CPE)
-
-            @pl.when(c != chip)
-            def _():
-                rcopy(
-                    part.at[pl.ds(pl.multiple_of(c * RCH, 16), RCH)], prs.at[chip],
-                    s_prs.at[c], r_prs.at[chip], exp_dev(2 * c + core),
-                ).start()
-
-        loop(0, CPE, send)
-
-    loop(0, ELOC, part_step)
-    mine = pl.ds(pl.multiple_of(chip * RCH, 16), RCH)
-    prs[chip] = part[mine, :]
-
     def wait_sq(d):
         j = ex_peer(d)
         rcopy(sq_r.at[j], sq_r.at[j], s_sq.at[j], r_sq.at[j], exp_dev(j)).wait_recv()
@@ -383,45 +405,142 @@
 
     loop(1, G, send_inv)
 
+    place = (cx, cy)
+
+    def along(h, off):
+        return at_chip(off, 0)[2] if h == 0 else at_chip(0, off)[2]
+
+    def across(h, off):
+        return at_chip(0, off)[2] if h == 0 else at_chip(off, 0)[2]
+
+    def ring1(h, slot, src):
+        n = 6 * h + slot
+        return rcopy(src, in1.at[h, slot], s_p1.at[n], r_p1.at[n], along(h, 1 if slot < 3 else -1))
+
+    def block(e):
+        return pl.ds(pl.multiple_of(e * ESL, 16), ESL)
+
+    def part_step(i):
+        e = lax.rem(cx + 2 + 3 * i, 4)
+        xo = mm(sel[e], xall[...].reshape(G * GROUP, W)).astype(BF16)
+        xs = mm(sel[e], xsib[...].reshape(G * GROUP, W)).astype(BF16)
+        for f in range(4):
+            cols = slice(2 * f * QF, 2 * (f + 1) * QF)
+            part[f, block(e)] = (mm(xo, wg[e, 0, :, cols]) + mm(xs, wg[e, 1, :, cols])).astype(BF16)
+        for h in range(2):
+            role = lax.rem(e - place[h] + 4, 4)
+
+            @pl.when(role == 2)
+            def _():
+                ring1(h, 0, part.at[2 * h, block(e)]).start()
+                ring1(h, 3, part.at[2 * h + 1, block(e)]).start()
+
+            @pl.when(role == 1)
+            def _():
+                ring1(h, 1, part.at[2 * h + 1, block(e)]).start()
+
+            @pl.when(role == 3)
+            def _():
+                ring1(h, 4, part.at[2 * h, block(e)]).start()
+
+    loop(0, 4, part_step)
+
+    for h in range(2):
+        for i in range(2):
+            to = lax.rem(place[h] + (1, 3)[i], 4)
+            ring1(h, 3 * i, in1.at[h, 3 * i]).wait_recv()
+            mixed = part[2 * h + i, block(to)].astype(F32) + in1[h, 3 * i].astype(F32)
+            out1[h, i] = mixed.astype(BF16)
+            ring1(h, 2 + 3 * i, out1.at[h, i]).start()
+
+    def rows2(p):
+        return pl.ds(pl.multiple_of(p * QR, 16), QR)
+
+    def ring2(h, off):
+        to = lax.rem(place[1 - h] + off, 4)
+        n = 3 * h + off - 1
+        return rcopy(
+            b2.at[h, :, rows2(to)], in2.at[h, 4 - off], s_p2.at[n], r_p2.at[n], across(h, off)
+        )
+
+    for h in range(2):
+        for i in range(2):
+            ring1(h, 4 - 3 * i, in1.at[h, 4 - 3 * i]).wait_recv()
+            ring1(h, 2 + 3 * i, in1.at[h, 2 + 3 * i]).wait_recv()
+            own = part[2 * h + i, block(place[h])].astype(F32)
+            got = in1[h, 4 - 3 * i].astype(F32) + in1[h, 2 + 3 * i].astype(F32)
+            b2[h, i] = (own + got).astype(BF16)
+        for off in (2, 1, 3):
+            ring2(h, off).start()
+        in2[h, 0] = b2[h, :, rows2(place[1 - h])]
+
     def wait_inv(d):
         j = dp_peer(d)
         rcopy(inv_r.at[j], inv_r.at[j], s_inv.at[j], r_inv.at[j], dp_dev(j)).wait_recv()
 
     loop(1, G, wait_inv)
     irow = jnp.concatenate([inv_r[j, 0:1, 0:GROUP] for j in range(G)], axis=1)
-    my_sel = sel[lax.div(chip, CPE), pl.ds(pl.multiple_of(lax.rem(chip, CPE) * RCH, 16), RCH), :]
-    icol = jnp.sum(my_sel.astype(F32) * irow, axis=1, keepdims=True)
-
-    def wait_prs(d):
-        c = chip_peer(d)
-        rcopy(prs.at[c], prs.at[c], s_prs.at[c], r_prs.at[c], exp_dev(2 * c + core)).wait_recv()
-
-    loop(1, NC, wait_prs)
-    tot = prs[0].astype(F32)
-    for c in range(1, NC):
-        tot = tot + prs[c].astype(F32)
-    tot = tot * icol
-    ga = tot[:, 0:FH]
-    hid[mine, :] = (ga / (1.0 + jnp.exp(-ga)) * tot[:, FH : 2 * FH]).astype(BF16)
-
-    def send_hid(d):
-        c = chip_peer(d)
-        rcopy(hid.at[mine], hid.at[mine], s_hid.at[c], r_hid.at[chip], exp_dev(2 * c + core)).start()
-
-    loop(1, NC, send_hid)
+
+    def hid_rows(h, x, y):
+        p = (x, y)
+        return pl.ds(pl.multiple_of(p[h] * ESL + p[1 - h] * QR, 16), QR)
+
+    for h in range(2):
+        mine = sel[place[h], rows2(place[1 - h]), :]
+        icol = jnp.sum(mine.astype(F32) * irow, axis=1, keepdims=True)
+        for off in (1, 3, 2):
+            ring2(h, off).wait_recv()
+        for i in range(2):
+            tot = in2[h, 0, i].astype(F32)
+            for j in range(1, 4):
+                tot = tot + in2[h, j, i].astype(F32)
+            tot = tot * icol
+            ga = tot[:, 0:QF]
+            hv = ga / (1.0 + jnp.exp(-ga)) * tot[:, QF : 2 * QF]
+            hid[2 * h + i, hid_rows(h, cx, cy)] = hv.astype(BF16)
+
+    def hid_send(n, h, src_x, src_y, dev):
+        ref = hid.at[pl.ds(2 * h, 2), hid_rows(h, src_x, src_y)]
+        return rcopy(ref, ref, s_hid.at[n], r_hid.at[2 * (4 * src_y + src_x) + h], dev)
+
+    def hid_quarter(n, f, src_x, src_y, dev):
+        ref = hid.at[f, hid_rows(f // 2, src_x, src_y)]
+        return rcopy(ref, ref, s_hid.at[n], r_hid.at[32 + f], dev)
+
+    around = [(1, 1), (1, -1), (-1, 1), (-1, -1), (1, 0), (-1, 0), (0, 1), (0, -1)]
+    hid_sends = []
+
+    def begin(c):
+        c.start()
+        hid_sends.append(c)
+
+    for ox, oy in around:
+        for h in range(2):
+            begin(hid_send(len(hid_sends), h, cx, cy, at_chip(ox, oy)[2]))
+    for ox, oy in around:
+        sx, sy, dev = at_chip(ox, oy)
+        for h in range(2):
+            hid_send(0, h, sx, sy, dev).wait_recv()
+        if ox != 0 and oy != 0:
+            f = (ox > 0) + 2 * (oy > 0)
+            begin(hid_quarter(len(hid_sends), f, sx, sy, at_chip(-ox, -oy)[2]))
+        if ox != 0:
+            begin(hid_send(len(hid_sends), int(ox > 0), sx, sy, at_chip(-ox, 0)[2]))
+        if oy != 0:
+            begin(hid_send(len(hid_sends), int(oy > 0), sx, sy, at_chip(0, -oy)[2]))
     c_wout.wait()
     rcopy(wout.at[1], wout.at[1], s_w.at[1], r_w.at[1], exp_dev(sib)).wait_recv()
-
-    def wait_hid(d):
-        c = chip_peer(d)
-        at = pl.ds(pl.multiple_of(c * RCH, 16), RCH)
-        rcopy(hid.at[at], hid.at[at], s_hid.at[c], r_hid.at[c], exp_dev(2 * c + core)).wait_recv()
-
-    loop(1, NC, wait_hid)
+    for ox, oy in ((2, 0), (2, 1), (2, -1), (0, 2), (1, 2), (-1, 2)):
+        sx, sy, dev = at_chip(ox, oy)
+        for h in range(2):
+            hid_send(0, h, sx, sy, dev).wait_recv()
+    sx, sy, dev = at_chip(2, 2)
+    for f in range(4):
+        hid_quarter(0, f, sx, sy, dev).wait_recv()
 
     def down(e):
         at = pl.ds(pl.multiple_of(e * ESL, 16), ESL)
-        he = hid[at, :]
+        he = jnp.concatenate([hid[f, at] for f in range(4)], axis=1)
         gs = gcol[e, :, 0:1]
         vsib[at, :] = (mm_nt(he, wout[1, e]) * gs).astype(BF16)
         vown[at, :] = (mm_nt(he, wout[0, e]) * gs).astype(BF16)
@@ -461,7 +580,6 @@
         j = dp_peer(d)
         dev = dp_dev(j)
         rcopy(sml_s.at[j], sml_r.at[g], s_sml.at[j], r_sml.at[g], dev).wait_send()
-        rcopy(q_all.at[g], q_all.at[g], s_q.at[j], r_q.at[g], dev).wait_send()
         rcopy(lse_s.at[j], lse_r.at[g], s_lse.at[j], r_lse.at[g], dev).wait_send()
         rcopy(hv_s.at[j], hv_r.at[g], s_hv.at[j], r_hv.at[g], dev).wait_send()
         rcopy(xall.at[g], xall.at[g], s_x.at[j], r_x.at[g], dev).wait_send()
@@ -483,14 +601,13 @@
 
     loop(0, G, drain_fw)
 
-    def drain_ch(d):
-        c = chip_peer(d)
-        dev = exp_dev(2 * c + core)
-        at = pl.ds(pl.multiple_of(c * RCH, 16), RCH)
-        rcopy(part.at[at], prs.at[chip], s_prs.at[c], r_prs.at[chip], dev).wait_send()
-        rcopy(hid.at[mine], hid.at[mine], s_hid.at[c], r_hid.at[chip], dev).wait_send()
-
-    loop(1, NC, drain_ch)
+    for c in q_sends + hid_sends:
+        c.wait_send()
+    for h in range(2):
+        for slot in range(6):
+            ring1(h, slot, in1.at[h, slot]).wait_send()
+        for off in (1, 2, 3):
+            ring2(h, off).wait_send()
 
 
 def body(
@@ -504,12 +621,11 @@
     GROUP, W = residual.shape
     ELOC, _, _, FF = expert_in.shape
     FH = FF // 2
-    NC = C // 2
     RH = ROWS * H
     capacity = min(GROUP, (3 * GROUP * TOP + 2 * G * ELOC - 1) // (2 * G * ELOC))
     ESL = G * capacity
     SLOTS = ELOC * ESL
-    RCH = SLOTS // NC
+    BLK, QR, QC = SLOTS // 4, SLOTS // 16, FF // 4
     N2 = G * RH
     ROWN = G * GROUP
 
@@ -518,20 +634,22 @@
 
     dma = lambda n: pltpu.SemaphoreType.DMA((n,))
     scratch = [
-        v((LAT, NS * PAGE)), v((NS * PAGE, KVR)), v((128, LAT)), v((G, ROWS, H, LAT)),
-        v((G, 16, 128), F32), v((G, 16, 128), F32), v((N2, N2)), v((N2, N2)),
-        v((N2, KVR)), v((N2, KVR)), v((N2, DV)), v((G, RH, DV)), v((G, 8, 128), F32),
-        v((G, RH, DV)), v((G, 8, 128), F32),
+        v((LAT, NS * PAGE)), v((NS * PAGE, KVR)), v((128, LAT)), v((ROWS, H, LAT)),
+        v((G, ROWS, H, -(-(LAT + 2) // 128) * 128)),
+        v((G, 8, 128), F32), v((G, 8, 128), F32), v((N2, N2)), v((N2, N2)),
+        v((N2, KVR)), v((N2, KVR)), v((N2, DV)), v((G, RH, DV)), v((G, 1, 128), F32),
+        v((G, RH, DV)), v((G, 1, 128), F32),
         v((C, RH, DV)), v((GROUP, H * DV)), v((H, KVR, DV)), v((W, H * DV)),
         v((2, ELOC, W, 2, FH)), v((ELOC, 2, W, FF)), v((2, ELOC, W, FH)),
-        v((G, GROUP, W)), v((G, GROUP, W)), v((8, 128), F32), v((C, 8, 128), F32),
-        v((8, 128), F32), v((G, 8, 128), F32),
+        v((G, GROUP, W)), v((G, GROUP, W)), v((1, 128), F32), v((C, 1, 128), F32),
+        v((1, 128), F32), v((G, 1, 128), F32),
         v((ELOC, ESL, ROWN)), v((ROWN, SLOTS)), v((ELOC, ESL, 128), F32),
-        v((SLOTS, FF)), v((NC, RCH, FF)), v((SLOTS, FH)), v((SLOTS, W)), v((SLOTS, W)),
+        v((4, SLOTS, QC)), v((2, 6, BLK, QC)), v((2, 2, BLK, QC)), v((2, 2, BLK, QC)),
+        v((2, 4, 2, QR, QC)), v((4, SLOTS, QC // 2)), v((SLOTS, W)), v((SLOTS, W)),
         v((ROWN, W)), v((ROWN, W)), v((G, GROUP, W)), v((G, GROUP, W)), v((ROWN, W), F32),
         dma(NS + 5),
     ]
-    for n in (G, G, G, G, G, G, G, C, C, NC, NC, G, 3):
+    for n in (G + 2, G, G, G, G, G, G, C, C, 12, 6, C + 4, G, 3):
         scratch += [dma(n), dma(n)]
     vm = pl.BlockSpec(memory_space=pltpu.VMEM)
     sm = pl.BlockSpec(memory_space=pltpu.SMEM)

time: 114 us -> 95.8 us (0.84)
  Pallas kernels: 112 us -> 94.2 us
    pallas_call x1, Pallas kernels: 112 us -> 94.2 us  [body(): pl.pallas_call(functools.partial(kernel, G, C, ELOC, capacity), out_shape...]
where the time goes in v2:
time: 95.8 us; the launch traced here: 95.6 us
  Pallas kernels  94.2 us (98%)
  local copies, waits for them, and re-layouts  1.38 us (1%)
    pallas_call x1, Pallas kernels, body(): pl.pallas_call(functools.partial(kernel, G, C, ELOC, capacity), out_shape...  94.2 us

profile of v2, /device:TPU:1, one launch (start us, length us, event | category | flops | bytes accessed | tf_op | source)
XLA Modules:
  0.0 95.6 jit_solution(11283163128711695764)
XLA Ops:
  0.0 94.2 %decode_step.1 = bf16[64,224]{1,0:T(8,128)(2,1)} custom-call(bf16[2,32,576]{2,1,0:T(8,128)(2,1)} %q_hbm.1, bf16[2,576]{1,0:T(2,128)(2,1)} %nl_ref.1, bf16[6,576,128]{2,1,0:T(8,128)(2,1)} %pool_hbm.1, s32[8,1,2,8]{3,2,1,0:T(2,128)} %owner_ref.1, s32[8,1,2,8]{3,2,1,0:T(2,128)} %slot_ref.1, s32[2]{0:T(128)} %len_ref.1, bf16[64,224]{1,0:T(8,128)(2,1)} %res_ref.1, ...), custom_call_target="tpu_custom_call" | custom-call | flops 4294967296 | bytes 16777216 | tf_op jit(solution)/shard_map/decode_step/pallas_call | solution.py:657
  94.2 1.4 %copy.16 = bf16[64,224]{1,0:T(8,128)(2,1)} copy(bf16[64,224]{1,0:T(8,128)(2,1)} %decode_step.1) | data formatting | bytes 57344

commit v3 on v2

v3 whole, which is shorter than its diff:
```python
import functools
import jax
import jax.numpy as jnp
from jax import lax
from jax.experimental import pallas as pl
from jax.experimental.pallas import tpu as pltpu
from jax.sharding import PartitionSpec as P

D = 7168
KVR = 512
ROPE = 64
DV = 128
TOP = 8
EPS = 1e-06
MESH = pl.DeviceIdType.MESH
F32 = jnp.float32
BF16 = jnp.bfloat16
NEG = -1e30
WAVES = ((0, 1, -1, 2), (-2, 3, -3, 4))
POS = {off: 4 * w + t for w in range(2) for t, off in enumerate(WAVES[w])}
BACK = {off: POS[4 if off == 4 else -off] for off in POS}


def iota(shape, dim):
    return lax.broadcasted_iota(jnp.int32, shape, dim)


def mm(a, b):
    return jnp.dot(a, b, preferred_element_type=F32)


def mm_nt(a, b):
    return lax.dot_general(a, b, (((1,), (1,)), ((), ())), preferred_element_type=F32)


def kernel(
    G, C, ELOC, CAPX,
    q_hbm, nl_hbm, pool_hbm, owner_hbm, slot_hbm, len_hbm, res_hbm, wv_hbm, wo_hbm, gain_hbm,
    ids_hbm, gates_hbm, win_hbm, wout_hbm,
    out_ref,
    nl_ref, owner_ref, slot_ref, len_ref, res_ref, gain_ref, ids_ref, gates_ref,
    kc, vt, nlp, q_in, q_all, sml_s, sml_r, perm, perm_t, o_all, o_hm, hv_hm, hv_s, lse_s, hv_r,
    lse_r, hva, xmat, wv, wo, win, wg, wout, xall, xsib, sq_s, sq_r, inv_s, inv_r,
    sel, sel_t, gcol, part, in1, out1, b2, in2, hid, vown, vsib, zsib_s, zsib_r, zs, zr, zown,
    lsem, sent, heard, r_q, r_x, r_hva, r_p1, r_p2, r_hid,
):
    g = lax.axis_index("dp")
    k = lax.axis_index("expert")
    core = lax.rem(k, 2)
    chip = lax.div(k, 2)
    sib = k + 1 - 2 * core
    cx = lax.rem(chip, 4)
    cy = lax.div(chip, 4)
    ROWS, H, LAT = q_in.shape
    NS = pool_hbm.shape[0]
    PAGE = pool_hbm.shape[2]
    RH = ROWS * H
    GROUP = C * ROWS
    W = res_ref.shape[1]
    FF = win_hbm.shape[3]
    FH = FF // 2
    ESL = 4 * CAPX
    QR = ESL // 2
    QF = FH // 4
    NR = G * ROWS

    def dp_peer(d):
        half = lax.div(G + 1 - d, 2)
        off = half * (1 - 2 * lax.rem(G + 1 - d, 2))
        return lax.rem(g + off + G, G)

    def at_dp(off):
        return lax.rem(g + off + G, G)

    def ex_peer(d):
        return lax.rem(k + d, C)

    def at_chip(ox, oy):
        x = lax.rem(cx + ox + 4, 4)
        y = lax.rem(cy + oy + 4, 4)
        return x, y, (g, 2 * (4 * y + x) + core)

    s_q, s_sml, s_hv, s_lse, s_hva, s_x, s_fw, s_sq = (sent.at[i] for i in range(8))
    s_inv, s_p1, s_p2, s_hid, s_win, s_wout, s_zsib, s_z = (sent.at[8 + i] for i in range(8))
    r_sml, r_hv, r_lse, r_inv, r_z, r_sq, r_win, r_wout = (heard.at[i] for i in range(8))
    r_fwd, r_sib, r_zsib = (heard.at[8], heard.at[9]), heard.at[10], (heard.at[11], heard.at[12])

    def rcopy(src, dst, ss, rs, dev):
        return pltpu.make_async_remote_copy(
            src_ref=src, dst_ref=dst, send_sem=ss, recv_sem=rs, device_id=dev, device_id_type=MESH
        )

    def sent_all(ref, sem):
        rcopy(ref, ref, sem, sem, exp_dev(sib)).wait_send()

    def heard_all(ref, sem):
        rcopy(ref, ref, sem, sem, exp_dev(sib)).wait_recv()

    def loop(lo, hi, fn):
        lax.fori_loop(lo, hi, lambda i, c: (fn(i), c)[1], 0)

    def exp_dev(kk):
        return (g, kk)

    def dp_dev(j):
        return (j, k)

    locals_ = []
    for s in range(NS):
        locals_.append(
            pltpu.make_async_copy(pool_hbm.at[s], kc.at[:, pl.ds(s * PAGE, PAGE)], lsem.at[0])
        )
    c_q = pltpu.make_async_copy(q_hbm, q_in, lsem.at[1])
    c_win = pltpu.make_async_copy(
        win_hbm.at[:, :, :, pl.ds(pl.multiple_of(core * FH, FH), FH)], win.at[0], lsem.at[2]
    )
    c_wv = pltpu.make_async_copy(wv_hbm, wv, lsem.at[3])
    c_wo = pltpu.make_async_copy(wo_hbm, wo, lsem.at[4])
    c_wout = pltpu.make_async_copy(
        wout_hbm.at[:, :, pl.ds(pl.multiple_of(core * FH, FH), FH)], wout.at[0], lsem.at[5]
    )
    c_q.start()
    small = []
    for i, (a, b) in enumerate(
        (
            (ids_hbm, ids_ref), (gates_hbm, gates_ref), (len_hbm, len_ref), (nl_hbm, nl_ref),
            (owner_hbm, owner_ref), (slot_hbm, slot_ref), (res_hbm, res_ref), (gain_hbm, gain_ref),
        )
    ):
        small.append(pltpu.make_async_copy(a, b, lsem.at[6 + i]))
        small[-1].start()
    for c in locals_:
        c.start()
    for c in (c_win, c_wv, c_wo, c_wout):
        c.start()

    barrier = pltpu.get_barrier_semaphore()

    def sig_dp(d):
        pl.semaphore_signal(barrier, inc=1, device_id=dp_dev(lax.rem(g + d, G)), device_id_type=MESH)

    def sig_ex(d):
        pl.semaphore_signal(barrier, inc=1, device_id=exp_dev(ex_peer(d)), device_id_type=MESH)

    loop(1, G, sig_dp)
    loop(1, C, sig_ex)

    for c in small:
        c.wait()
    ids = ids_ref[...]
    gates = gates_ref[...]
    e_iota = iota((G * ELOC, GROUP), 0)
    named = jnp.zeros((G * ELOC, GROUP), F32)
    gval = jnp.zeros((G * ELOC, GROUP), F32)
    for t in range(TOP):
        hit = ids[t : t + 1, :] == e_iota
        named = named + hit.astype(F32)
        gval = gval + jnp.where(hit, gates[t : t + 1, :], 0.0)
    tri = (iota((GROUP, GROUP), 0) < iota((GROUP, GROUP), 1)).astype(BF16)
    rank = mm(named.astype(BF16), tri)
    code = jnp.where(named > 0, rank, -1.0)
    sml_s[...] = jnp.zeros_like(sml_s)
    for j in range(G):
        sml_s[j, 0:ELOC, 0:GROUP] = code[j * ELOC : (j + 1) * ELOC]
        sml_s[j, ELOC : 2 * ELOC, 0:GROUP] = gval[j * ELOC : (j + 1) * ELOC]
    sml_r[0] = sml_s[g]

    N2 = NR * H
    pr = iota((N2, 1), 0)
    perm[...] = (iota((N2, N2), 1) == lax.rem(pr, NR) * H + lax.div(pr, NR)).astype(BF16)
    perm_t[...] = (iota((N2, N2), 1) == lax.rem(pr, H) * NR + lax.div(pr, H)).astype(BF16)
    nl = nl_ref[...].astype(F32)
    nrow = iota((128, LAT), 0)
    nacc = jnp.zeros((128, LAT), F32)
    for s in range(ROWS):
        nacc = jnp.where(nrow == s, nl[s : s + 1, :], nacc)
    nlp[...] = nacc.astype(BF16)

    c_q.wait()
    for r in range(ROWS):
        n = len_ref[r]
        li = iota((H, q_all.shape[3] - LAT), 1)
        tail = jnp.where(li == 0, lax.div(n, 32), jnp.where(li == 1, lax.rem(n, 32), 0))
        q_all[g, r] = jnp.concatenate([q_in[r], tail.astype(F32).astype(BF16)], axis=1)
    pl.semaphore_wait(barrier, G - 1 + C - 1)

    def q_copy(src, off, row=None):
        ref = q_all.at[src] if row is None else q_all.at[src, row]
        return rcopy(ref, ref, s_q, r_q.at[src], dp_dev(at_dp(off)))

    for off in (2, -2, 1, -1):
        q_copy(g, off).start()

    other = pl.multiple_of((1 - core) * FH, FH)
    w1 = rcopy(win_hbm.at[:, :, :, pl.ds(other, FH)], win.at[1], s_win, r_win, exp_dev(sib))
    w2 = rcopy(wout_hbm.at[:, :, pl.ds(other, FH)], wout.at[1], s_wout, r_wout, exp_dev(sib))
    w1.start()
    w2.start()

    pltpu.make_async_copy(kc, kc, lsem.at[0]).wait()
    vt[...] = kc[0:KVR, :].T

    scale = (DV + ROPE) ** (-0.5)
    NT = NS * PAGE

    def attend(src, own):
        qx = q_all[src].reshape(RH, q_all.shape[3])
        q = qx[:, 0:LAT]
        sc = mm(q, kc[...]) * scale
        lid = iota((1, NT), 1)
        slot_lane = lax.div(lid, PAGE)
        tpos = lax.rem(lid, PAGE).astype(F32)
        rows = []
        for s in range(ROWS):
            lv = qx[s * H : s * H + 8, LAT : LAT + 2].astype(F32)
            ln = lv[0:1, 0:1] * 32.0 + lv[0:1, 1:2]
            cnt = jnp.zeros((1, NT), F32)
            for p in range(owner_ref.shape[3]):
                here = jnp.where(owner_ref[src, 0, s, p] == g, slot_ref[src, 0, s, p], -1)
                ok = jnp.logical_and(slot_lane == here, tpos + float(p * PAGE) < ln)
                cnt = cnt + ok.astype(F32)
            rows.append(jnp.broadcast_to(cnt, (H, NT)))
        cnt = jnp.concatenate(rows, axis=0)
        scm = jnp.where(cnt > 0, sc, NEG)
        top = jnp.max(scm, axis=1, keepdims=True)
        if own:
            cs = (iota((RH, 128), 1) == lax.div(iota((RH, 128), 0), H)).astype(F32)
            ss = jnp.where(cs > 0, mm_nt(q, nlp[...]) * scale, NEG)
            top = jnp.maximum(top, jnp.max(ss, axis=1, keepdims=True))
        p = cnt * jnp.exp(scm - top)
        den = jnp.sum(p, axis=1, keepdims=True)
        acc = mm(p.astype(BF16), vt[...])
        if own:
            pself = cs * jnp.exp(ss - top)
            den = den + jnp.sum(pself, axis=1, keepdims=True)
            acc = acc + mm(pself.astype(BF16), nlp[:, 0:KVR])
        has = den > 0
        inv_den = jnp.where(has, 1.0 / jnp.where(has, den, 1.0), 0.0)
        lse = jnp.where(has, top + jnp.log(jnp.where(has, den, 1.0)), NEG)
        o_all[pl.ds(pl.multiple_of(src * RH, RH), RH), :] = (acc * inv_den).astype(BF16)
        row = jnp.broadcast_to(lse, (RH, 128)).T[0:1]
        lse_s[src] = jnp.concatenate([row, row], axis=1)

    attend(g, True)

    col = iota((W, 2 * W), 1)
    two = 2 * iota((W, 2 * W), 0)
    pick_g = (col == two).astype(BF16)
    pick_u = (col == two + 1).astype(BF16)

    def split(o, e):
        w = win[o, e].reshape(2 * W, FH)
        wgate = mm(pick_g, w).astype(BF16)
        wup = mm(pick_u, w).astype(BF16)
        for f in range(4):
            wg[e, o, :, 2 * f * QF : (2 * f + 1) * QF] = wgate[:, f * QF : (f + 1) * QF]
            wg[e, o, :, (2 * f + 1) * QF : 2 * (f + 1) * QF] = wup[:, f * QF : (f + 1) * QF]

    c_win.wait()
    loop(0, ELOC, lambda e: split(0, e))

    for i, off in ((0, -2), (1, 2)):
        src = at_dp(off)
        q_copy(src, off).wait_recv()
        q_copy(src, 1 - 2 * i).start()
        q_copy(src, 2 - 4 * i, row=i).start()

    def sml_copy(off, n):
        j = at_dp(off)
        return rcopy(sml_s.at[j], sml_r.at[n], s_sml, r_sml, dp_dev(j))

    others = [4, -3, 3, -2, 2, -1, 1]
    for off in others:
        sml_copy(off, BACK[off]).start()

    def ring(d):
        n = lax.div(d, 2)
        m = jnp.where(n == 0, 2, jnp.where(n == 1, 1, n + 1))
        return at_dp(jnp.where(lax.rem(d, 2) == 0, -m, m))

    def near(d):
        attend(ring(d), False)

    def chunk(d):
        src = ring(d)
        heard_all(q_all.at[src], r_q.at[src])
        attend(src, False)

    loop(0, 2, near)
    loop(2, G - 2, chunk)
    far = at_dp(G // 2)
    heard_all(q_all.at[far], r_q.at[far])
    attend(far, False)

    o_hm[...] = mm(perm[...], o_all[...]).astype(BF16)
    c_wv.wait()
    HB = 8

    def project(b):
        for i in range(HB):
            h = b * HB + i
            at = pl.ds(pl.multiple_of(h * NR, NR), NR)
            hv_hm[at, :] = mm(o_hm[at, :], wv[h]).astype(BF16)

    loop(0, H // HB, project)
    hv_s[...] = mm(perm_t[...], hv_hm[...]).astype(BF16).reshape(G, RH, DV)
    hv_r[g] = hv_s[g]
    lse_r[g] = lse_s[g]

    def send_hv(d):
        j = dp_peer(d)
        rcopy(lse_s.at[j], lse_r.at[g], s_lse, r_lse, dp_dev(j)).start()
        rcopy(hv_s.at[j], hv_r.at[g], s_hv, r_hv, dp_dev(j)).start()

    loop(1, G, send_hv)

    heard_all(win.at[1], r_win)
    loop(0, ELOC, lambda e: split(1, e))
    heard_all(sml_r.at[pl.ds(1, G - 1)], r_sml)
    siota = iota((ESL, 4 * GROUP), 0).astype(F32)
    for w in range(2):
        for e in range(ELOC):
            codes = []
            gvals = []
            for t in range(4):
                cj = sml_r[4 * w + t, e : e + 1, 0:GROUP]
                codes.append(jnp.where(cj >= 0, cj + float(t * CAPX), -1.0))
                gvals.append(sml_r[4 * w + t, ELOC + e : ELOC + e + 1, 0:GROUP])
            hit = siota == jnp.concatenate(codes, axis=1)
            sel[w, e] = hit.astype(F32).astype(BF16)
            gs = jnp.where(hit, jnp.concatenate(gvals, axis=1), 0.0)
            gcol[w, e] = jnp.broadcast_to(jnp.sum(gs, axis=1, keepdims=True), (ESL, 128))
        sel_t[w] = sel[w].reshape(ELOC * ESL, 4 * GROUP).T

    heard_all(lse_r.at[pl.ds(0, G - 1)], r_lse)
    heard_all(hv_r.at[pl.ds(0, G - 1)], r_hv)
    riota = iota((8, 128), 0)
    ls = jnp.full((8, 128), NEG, F32)
    for j in range(G):
        ls = jnp.where(riota == j, lse_r[j], ls)
    wts = jnp.exp(ls - jnp.max(ls, axis=0, keepdims=True))
    wts = wts / jnp.sum(wts, axis=0, keepdims=True)
    wcol = wts.T
    comb = jnp.zeros((RH, DV), F32)
    for j in range(G):
        comb = comb + wcol[0:RH, j : j + 1] * hv_r[j].astype(F32)
    hva[k] = comb.astype(BF16)

    plane = [(2, 2), (2, 1), (2, -1), (1, 2), (-1, 2), (2, 0), (0, 2)]
    plane += [(1, 1), (1, -1), (-1, 1), (-1, -1), (1, 0), (-1, 0), (0, 1), (0, -1)]
    for ox, oy in plane:
        rcopy(hva.at[k], hva.at[k], s_hva, r_hva.at[chip], at_chip(ox, oy)[2]).start()
    rcopy(hva.at[k], hva.at[k], s_hva, r_sib, exp_dev(sib)).start()
    for ox, oy in plane[::-1]:
        sx, sy, dev = at_chip(ox, oy)
        c = 4 * sy + sx
        got = hva.at[2 * c + core]
        heard_all(got, r_hva.at[c])
        rcopy(got, got, s_hva, r_sib, exp_dev(sib)).start()
    c_wo.wait()
    heard_all(hva.at[pl.ds(0, C // 2)], r_sib)

    for b in range(C // G):
        blk = mm(perm[...], hva[b * G : (b + 1) * G].reshape(N2, DV)).astype(BF16)
        for h in range(H):
            xmat[b * NR : (b + 1) * NR, h * DV : (h + 1) * DV] = blk[h * NR : (h + 1) * NR]
    proj = mm_nt(xmat[...], wo[...])
    resid = (res_ref[...].astype(F32) + proj).astype(BF16).astype(F32)
    xall[0, 0] = (resid * gain_ref[...]).astype(BF16)

    def x_copy(off, n):
        ref = xall.at[n // 4, n % 4]
        return rcopy(xall.at[0, 0], ref, s_x, r_x.at[n], dp_dev(at_dp(off)))

    def fwd(n):
        src, dst = xall.at[n // 4, n % 4], xsib.at[n // 4, n % 4]
        return rcopy(src, dst, s_fw, r_fwd[n // 4], exp_dev(sib))

    for off in (-1, 1, -2, 4, -3, 3, 2):
        x_copy(off, BACK[off]).start()
    fwd(0).start()
    sq = jnp.sum(resid * resid, axis=1, keepdims=True)
    sq_row = jnp.broadcast_to(sq, (GROUP, 128)).T[0:1]
    sq_s[...] = jnp.concatenate([sq_row] * (128 // GROUP), axis=1)
    sq_r[k] = sq_s[...]

    def send_sq(d):
        j = ex_peer(d)
        rcopy(sq_s, sq_r.at[k], s_sq, r_sq, exp_dev(j)).start()

    loop(1, C, send_sq)

    def get_x(w):
        for off in sorted(WAVES[w], key=abs):
            if off != 0:
                x_copy(off, POS[off]).wait_recv()
                fwd(POS[off]).start()
        heard_all(xsib.at[w], r_fwd[w])

    place = (cx, cy)

    def along(h, off):
        return at_chip(off, 0)[2] if h == 0 else at_chip(0, off)[2]

    def across(h, off):
        return at_chip(0, off)[2] if h == 0 else at_chip(off, 0)[2]

    def ring1(w, h, slot, src):
        sem = r_p1.at[3 * (2 * w + h) + min(slot, 2)]
        return rcopy(src, in1.at[w, h, slot], s_p1, sem, along(h, 1 if slot in (0, 2, 3) else -1))

    def block(e):
        return pl.ds(pl.multiple_of(e * ESL, 16), ESL)

    def partials(w):
        def step(i):
            e = lax.rem(cx + 2 + 3 * i, 4)
            xo = mm(sel[w, e], xall[w].reshape(4 * GROUP, W)).astype(BF16)
            xs = mm(sel[w, e], xsib[w].reshape(4 * GROUP, W)).astype(BF16)
            for f in range(4):
                cols = slice(2 * f * QF, 2 * (f + 1) * QF)
                both = mm(xo, wg[e, 0, :, cols]) + mm(xs, wg[e, 1, :, cols])
                part[w, f, block(e)] = both.astype(BF16)
            for h in range(2):
                role = lax.rem(e - place[h] + 4, 4)

                @pl.when(role == 2)
                def _():
                    ring1(w, h, 0, part.at[w, 2 * h, block(e)]).start()
                    ring1(w, h, 1, part.at[w, 2 * h + 1, block(e)]).start()

                @pl.when(role == 1)
                def _():
                    ring1(w, h, 2, part.at[w, 2 * h + 1, block(e)]).start()

                @pl.when(role == 3)
                def _():
                    ring1(w, h, 4, part.at[w, 2 * h, block(e)]).start()

        loop(0, 4, step)

    def relay(w):
        for h in range(2):
            for i in range(2):
                to = lax.rem(place[h] + (1, 3)[i], 4)
                ring1(w, h, i, in1.at[w, h, i]).wait_recv()
                passed = part[w, 2 * h + i, block(to)].astype(F32) + in1[w, h, i].astype(F32)
                out1[w, h, i] = passed.astype(BF16)
                ring1(w, h, 3 + 2 * i, out1.at[w, h, i]).start()

    def rows2(p):
        return pl.ds(pl.multiple_of(lax.div(p, 2) * QR, 16), QR)

    def ring2(w, h, off):
        to = lax.rem(place[1 - h] + off, 4)
        src = b2.at[w, h, lax.rem(to, 2), rows2(to)]
        return rcopy(src, in2.at[w, h, 4 - off], s_p2, r_p2.at[2 * w + h], across(h, off))

    def second(w):
        for h in range(2):
            heard_all(in1.at[w, h, pl.ds(2, 4)], r_p1.at[3 * (2 * w + h) + 2])
            for i in range(2):
                own = part[w, 2 * h + i, block(place[h])].astype(F32)
                got = in1[w, h, 4 - 2 * i].astype(F32) + in1[w, h, 3 + 2 * i].astype(F32)
                b2[w, h, i] = (own + got).astype(BF16)
            for off in (2, 1, 3):
                ring2(w, h, off).start()
            p = place[1 - h]
            in2[w, h, 0] = b2[w, h, lax.rem(p, 2), rows2(p)]

    def piece(w, h, x, y):
        p = (x, y)
        at = p[h] * ESL + lax.div(p[1 - h], 2) * QR
        return w, 2 * h + lax.rem(p[1 - h], 2), pl.ds(pl.multiple_of(at, 16), QR)

    around = [(1, 1), (1, -1), (-1, 1), (-1, -1), (1, 0), (-1, 0), (0, 1), (0, -1)]

    def hid_copy(w, h, sx, sy, n, dev):
        ref = hid.at[piece(w, h, sx, sy)]
        return rcopy(ref, ref, s_hid, r_hid.at[9 * w + n], dev)

    def hidden(w):
        irow = jnp.concatenate([inv_r[4 * w + t, 0:1, 0:GROUP] for t in range(4)], axis=1)
        for h in range(2):
            mine = sel[w, place[h], rows2(place[1 - h]), :]
            icol = jnp.sum(mine.astype(F32) * irow, axis=1, keepdims=True)
            heard_all(in2.at[w, h, pl.ds(1, 3)], r_p2.at[2 * w + h])
            tot = in2[w, h, 0].astype(F32)
            for j in range(1, 4):
                tot = tot + in2[w, h, j].astype(F32)
            tot = tot * icol
            ga = tot[:, 0:QF]
            hv = ga / (1.0 + jnp.exp(-ga)) * tot[:, QF : 2 * QF]
            hid[piece(w, h, cx, cy)] = hv.astype(BF16)
            for ox, oy in around:
                n = around.index((-ox, -oy))
                hid_copy(w, h, cx, cy, n, at_chip(ox, oy)[2]).start()

    def spread(w):
        for n, (ox, oy) in enumerate(around):
            sx, sy, _ = at_chip(ox, oy)
            heard_all(hid.at[w, pl.ds(0, 2), pl.ds(0, QR)], r_hid.at[9 * w + n])
            if ox == oy:
                hid_copy(w, int(ox > 0), sx, sy, 8, at_chip(-ox, -oy)[2]).start()
            if ox != 0:
                hid_copy(w, int(ox > 0), sx, sy, 8, at_chip(-ox, 0)[2]).start()
            if oy != 0:
                hid_copy(w, int(oy > 0), sx, sy, 8, at_chip(0, -oy)[2]).start()

    def down(w):
        heard_all(hid.at[w, pl.ds(0, 2), pl.ds(0, 7 * QR)], r_hid.at[9 * w + 8])

        def step(e):
            at = block(e)
            he = jnp.concatenate([hid[w, f, at] for f in range(4)], axis=1)
            gs = gcol[w, e, :, 0:1]
            vsib[w, at, :] = (mm_nt(he, wout[1, e]) * gs).astype(BF16)
            vown[w, at, :] = (mm_nt(he, wout[0, e]) * gs).astype(BF16)

        loop(0, ELOC, step)
        zsib_s[w] = mm(sel_t[w], vsib[w]).astype(BF16)
        zsib_copy(w).start()
        zown[w] = mm(sel_t[w], vown[w])

    def zsib_copy(w):
        return rcopy(zsib_s.at[w], zsib_r.at[w], s_zsib, r_zsib[w], exp_dev(sib))

    def z_copy(off, n):
        ref = zs.at[POS[off] // 4, POS[off] % 4]
        return rcopy(ref, zr.at[n], s_z, r_z, dp_dev(at_dp(off)))

    def give_back(w):
        zsib_copy(w).wait_recv()
        zsum = zown[w] + zsib_r[w].astype(F32)
        zown[w] = zsum
        zs[w] = zsum.astype(BF16).reshape(4, GROUP, W)
        for off in sorted(WAVES[w], key=lambda o: -abs(o)):
            if off != 0:
                z_copy(off, BACK[off]).start()

    get_x(0)
    partials(0)

    heard_all(sq_r.at[pl.ds(0, C - 1)], r_sq)
    inv_s[...] = lax.rsqrt(jnp.sum(sq_r[...], axis=0) / D + EPS)
    inv_r[0] = inv_s[...]

    def inv_copy(off, n):
        return rcopy(inv_s, inv_r.at[n], s_inv, r_inv, dp_dev(at_dp(off)))

    for off in others:
        inv_copy(off, BACK[off]).start()
    get_x(1)
    partials(1)
    relay(0)
    second(0)
    relay(1)
    heard_all(inv_r.at[pl.ds(1, G - 1)], r_inv)
    hidden(0)
    second(1)
    spread(0)
    hidden(1)
    c_wout.wait()
    heard_all(wout.at[1], r_wout)
    down(0)
    spread(1)
    give_back(0)
    down(1)
    give_back(1)
    total = resid + zown[0, 0:GROUP, :]

    w1.wait_send()
    w2.wait_send()
    seven = pl.ds(0, G - 1)
    sent_all(q_all.at[seven], s_q)
    sent_all(sml_r.at[seven], s_sml)
    sent_all(hv_r.at[seven], s_hv)
    sent_all(lse_r.at[seven], s_lse)
    sent_all(hva.at[pl.ds(0, C - 1)], s_hva)
    sent_all(zr.at[seven], s_x)
    sent_all(zr, s_fw)
    sent_all(sq_r.at[pl.ds(0, C - 1)], s_sq)
    sent_all(inv_r.at[seven], s_inv)
    sent_all(in1, s_p1)
    sent_all(in2.at[:, :, pl.ds(0, 3)], s_p2)
    sent_all(wv.at[pl.ds(0, 30), pl.ds(0, 2 * QR)], s_hid)
    sent_all(zsib_r, s_zsib)

    heard_all(zr.at[pl.ds(1, G - 1)], r_z)
    for n in range(1, G):
        total = total + zr[n].astype(F32)
    out_ref[...] = total.astype(BF16)
    sent_all(zr.at[seven], s_z)


def body(
    queries, new_latent, pool_pages, page_owner, page_slot, lengths, residual, value_weight,
    output_weight, norm_gain, expert_ids, route_gates, expert_in, expert_out,
):
    G = lax.axis_size("dp")
    C = lax.axis_size("expert")
    ROWS, H, LAT = queries.shape
    NS, _, PAGE = pool_pages.shape
    GROUP, W = residual.shape
    ELOC, _, _, FF = expert_in.shape
    FH = FF // 2
    RH = ROWS * H
    capacity = min(GROUP, (3 * GROUP * TOP + 2 * G * ELOC - 1) // (2 * G * ELOC))
    ESL = 4 * capacity
    SLOTS = ELOC * ESL
    QR, QC = ESL // 2, FF // 4
    N2 = G * RH
    HALF = 4 * GROUP

    def v(shape, dtype=BF16):
        return pltpu.VMEM(shape, dtype)

    dma = lambda n: pltpu.SemaphoreType.DMA((n,))
    scratch = [
        v(new_latent.shape), pltpu.SMEM(page_owner.shape, jnp.int32),
        pltpu.SMEM(page_slot.shape, jnp.int32), pltpu.SMEM(lengths.shape, jnp.int32),
        v((GROUP, W)), v((1, W), F32), v((TOP, GROUP), jnp.int32), v((TOP, GROUP), F32),
        v((LAT, NS * PAGE)), v((NS * PAGE, KVR)), v((128, LAT)), v((ROWS, H, LAT)),
        v((G, ROWS, H, -(-(LAT + 2) // 128) * 128)),
        v((G, 8, 128), F32), v((G, 8, 128), F32), v((N2, N2)), v((N2, N2)),
        v((N2, KVR)), v((N2, KVR)), v((N2, DV)), v((G, RH, DV)), v((G, 1, 128), F32),
        v((G, RH, DV)), v((G, 1, 128), F32),
        v((C, RH, DV)), v((GROUP, H * DV)), v((H, KVR, DV)), v((W, H * DV)),
        v((2, ELOC, W, 2, FH)), v((ELOC, 2, W, FF)), v((2, ELOC, W, FH)),
        v((2, 4, GROUP, W)), v((2, 4, GROUP, W)), v((1, 128), F32), v((C, 1, 128), F32),
        v((1, 128), F32), v((G, 1, 128), F32),
        v((2, ELOC, ESL, HALF)), v((2, HALF, SLOTS)), v((2, ELOC, ESL, 128), F32),
        v((2, 4, SLOTS, QC)), v((2, 2, 6, ESL, QC)), v((2, 2, 2, ESL, QC)), v((2, 2, 2, ESL, QC)),
        v((2, 2, 4, QR, QC)), v((2, 4, SLOTS, QC // 2)), v((2, SLOTS, W)), v((2, SLOTS, W)),
        v((2, HALF, W)), v((2, HALF, W)), v((2, 4, GROUP, W)), v((G, GROUP, W)),
        v((2, HALF, W), F32),
        dma(14), dma(16), dma(13), dma(G), dma(G), dma(C // 2), dma(12), dma(4), dma(18),
    ]
    vm = pl.BlockSpec(memory_space=pltpu.VMEM)
    hbm = pl.BlockSpec(memory_space=pl.ANY)
    return pl.pallas_call(
        functools.partial(kernel, G, C, ELOC, capacity),
        out_shape=jax.ShapeDtypeStruct((GROUP, W), BF16),
        in_specs=[hbm] * 14,
        out_specs=vm,
        scratch_shapes=scratch,
        compiler_params=pltpu.CompilerParams(
            collective_id=0, has_side_effects=True, vmem_limit_bytes=56 << 20
        ),
        cost_estimate=pl.CostEstimate(flops=4 << 30, bytes_accessed=16 << 20, transcendentals=1 << 20),
        name="decode_step",
    )(
        queries, new_latent, pool_pages, page_owner, page_slot, lengths, residual, value_weight,
        output_weight.T, norm_gain.reshape(1, W), expert_ids.T, route_gates.T, expert_in,
        jnp.swapaxes(expert_out, 1, 2),
    )


def solution(mesh):
    in_specs = (
        P(("dp", "expert"), None, None),
        P(("dp", "expert"), None),
        P(("dp", "expert"), None, None),
        P(None, "expert", None, None),
        P(None, "expert", None, None),
        P(("dp", "expert")),
        P("dp", "expert"),
        P(),
        P(None, "expert"),
        P("expert"),
        P("dp", None),
        P("dp", None),
        P("dp", "expert", None, None),
        P("dp", None, "expert"),
    )
    return jax.shard_map(
        body, mesh=mesh, in_specs=in_specs, out_specs=P("dp", "expert"), check_vma=False
    )
```

time: 95.8 us -> 86.7 us (0.905)
  Pallas kernels: 94.2 us -> 85.2 us
    pallas_call x1, Pallas kernels: 94.2 us -> 85.2 us  [body(): pl.pallas_call(functools.partial(kernel, G, C, ELOC, capacity), out_shape...]
where the time goes in v3:
time: 86.7 us; the launch traced here: 86.6 us
  Pallas kernels  85.2 us (98%)
  local copies, waits for them, and re-layouts  1.38 us (2%)
    pallas_call x1, Pallas kernels, body(): pl.pallas_call(functools.partial(kernel, G, C, ELOC, capacity), out_shape...  85.2 us

profile of v3, /device:TPU:1, one launch (start us, length us, event | category | flops | bytes accessed | tf_op | source)
XLA Modules:
  0.0 86.6 jit_solution(15671778399958930786)
XLA Ops:
  0.0 85.2 %decode_step.1 = bf16[64,224]{1,0:T(8,128)(2,1)} custom-call(bf16[2,32,576]{2,1,0:T(8,128)(2,1)} %q_hbm.1, bf16[2,576]{1,0:T(2,128)(2,1)} %nl_hbm.1, bf16[6,576,128]{2,1,0:T(8,128)(2,1)} %pool_hbm.1, s32[8,1,2,8]{3,2,1,0:T(2,128)} %owner_hbm.1, s32[8,1,2,8]{3,2,1,0:T(2,128)} %slot_hbm.1, s32[2]{0:T(128)} %len_hbm.1, bf16[64,224]{1,0:T(8,128)(2,1)} %res_hbm.1, ...), custom_call_target="tpu_custom_call" | custom-call | flops 4294967296 | bytes 16777216 | tf_op jit(solution)/shard_map/decode_step/pallas_call | solution.py:641
  85.2 1.4 %copy.16 = bf16[64,224]{1,0:T(8,128)(2,1)} copy(bf16[64,224]{1,0:T(8,128)(2,1)} %decode_step.1) | data formatting | bytes 57344

commit v4 on v3

--- a/solution.py
+++ b/solution.py
@@ -16,8 +16,9 @@
 F32 = jnp.float32
 BF16 = jnp.bfloat16
 NEG = -1e30
-WAVES = ((0, 1, -1, 2), (-2, 3, -3, 4))
+WAVES = ((4, -3, 3, -2), (0, 1, -1, 2))
 POS = {off: 4 * w + t for w in range(2) for t, off in enumerate(WAVES[w])}
+ME = POS[0]
 BACK = {off: POS[4 if off == 4 else -off] for off in POS}
 
 
@@ -42,7 +43,7 @@
     kc, vt, nlp, q_in, q_all, sml_s, sml_r, perm, perm_t, o_all, o_hm, hv_hm, hv_s, lse_s, hv_r,
     lse_r, hva, xmat, wv, wo, win, wg, wout, xall, xsib, sq_s, sq_r, inv_s, inv_r,
     sel, sel_t, gcol, part, in1, out1, b2, in2, hid, vown, vsib, zsib_s, zsib_r, zs, zr, zown,
-    lsem, sent, heard, r_q, r_x, r_hva, r_p1, r_p2, r_hid,
+    lsem, sent, heard, r_q, r_x, r_hva, r_sib, r_p1, r_p2, r_hid,
 ):
     g = lax.axis_index("dp")
     k = lax.axis_index("expert")
@@ -83,7 +84,7 @@
     s_q, s_sml, s_hv, s_lse, s_hva, s_x, s_fw, s_sq = (sent.at[i] for i in range(8))
     s_inv, s_p1, s_p2, s_hid, s_win, s_wout, s_zsib, s_z = (sent.at[8 + i] for i in range(8))
     r_sml, r_hv, r_lse, r_inv, r_z, r_sq, r_win, r_wout = (heard.at[i] for i in range(8))
-    r_fwd, r_sib, r_zsib = (heard.at[8], heard.at[9]), heard.at[10], (heard.at[11], heard.at[12])
+    r_fwd, r_zsib = (heard.at[8], heard.at[9]), (heard.at[10], heard.at[11])
 
     def rcopy(src, dst, ss, rs, dev):
         return pltpu.make_async_remote_copy(
@@ -145,8 +146,25 @@
     loop(1, G, sig_dp)
     loop(1, C, sig_ex)
 
-    for c in small:
-        c.wait()
+    c_q.wait()
+    small[2].wait()
+    for r in range(ROWS):
+        n = len_ref[r]
+        li = iota((H, q_all.shape[3] - LAT), 1)
+        tail = jnp.where(li == 0, lax.div(n, 32), jnp.where(li == 1, lax.rem(n, 32), 0))
+        q_all[g, r] = jnp.concatenate([q_in[r], tail.astype(F32).astype(BF16)], axis=1)
+    pl.semaphore_wait(barrier, G - 1 + C - 1)
+
+    def q_copy(src, off, row=None):
+        ref = q_all.at[src] if row is None else q_all.at[src, row]
+        return rcopy(ref, ref, s_q, r_q.at[src], dp_dev(at_dp(off)))
+
+    for off in (2, -2, 1, -1):
+        q_copy(g, off).start()
+
+    for i, c in enumerate(small):
+        if i != 2:
+            c.wait()
     ids = ids_ref[...]
     gates = gates_ref[...]
     e_iota = iota((G * ELOC, GROUP), 0)
@@ -163,7 +181,7 @@
     for j in range(G):
         sml_s[j, 0:ELOC, 0:GROUP] = code[j * ELOC : (j + 1) * ELOC]
         sml_s[j, ELOC : 2 * ELOC, 0:GROUP] = gval[j * ELOC : (j + 1) * ELOC]
-    sml_r[0] = sml_s[g]
+    sml_r[ME] = sml_s[g]
 
     N2 = NR * H
     pr = iota((N2, 1), 0)
@@ -175,21 +193,6 @@
     for s in range(ROWS):
         nacc = jnp.where(nrow == s, nl[s : s + 1, :], nacc)
     nlp[...] = nacc.astype(BF16)
-
-    c_q.wait()
-    for r in range(ROWS):
-        n = len_ref[r]
-        li = iota((H, q_all.shape[3] - LAT), 1)
-        tail = jnp.where(li == 0, lax.div(n, 32), jnp.where(li == 1, lax.rem(n, 32), 0))
-        q_all[g, r] = jnp.concatenate([q_in[r], tail.astype(F32).astype(BF16)], axis=1)
-    pl.semaphore_wait(barrier, G - 1 + C - 1)
-
-    def q_copy(src, off, row=None):
-        ref = q_all.at[src] if row is None else q_all.at[src, row]
-        return rcopy(ref, ref, s_q, r_q.at[src], dp_dev(at_dp(off)))
-
-    for off in (2, -2, 1, -1):
-        q_copy(g, off).start()
 
     other = pl.multiple_of((1 - core) * FH, FH)
     w1 = rcopy(win_hbm.at[:, :, :, pl.ds(other, FH)], win.at[1], s_win, r_win, exp_dev(sib))
@@ -294,7 +297,7 @@
 
     o_hm[...] = mm(perm[...], o_all[...]).astype(BF16)
     c_wv.wait()
-    HB = 8
+    HB = 16
 
     def project(b):
         for i in range(HB):
@@ -316,7 +319,7 @@
 
     heard_all(win.at[1], r_win)
     loop(0, ELOC, lambda e: split(1, e))
-    heard_all(sml_r.at[pl.ds(1, G - 1)], r_sml)
+    heard_all(sml_r.at[pl.ds(0, G - 1)], r_sml)
     siota = iota((ESL, 4 * GROUP), 0).astype(F32)
     for w in range(2):
         for e in range(ELOC):
@@ -350,35 +353,36 @@
     plane += [(1, 1), (1, -1), (-1, 1), (-1, -1), (1, 0), (-1, 0), (0, 1), (0, -1)]
     for ox, oy in plane:
         rcopy(hva.at[k], hva.at[k], s_hva, r_hva.at[chip], at_chip(ox, oy)[2]).start()
-    rcopy(hva.at[k], hva.at[k], s_hva, r_sib, exp_dev(sib)).start()
+    rcopy(hva.at[k], hva.at[k], s_hva, r_sib.at[cy], exp_dev(sib)).start()
     for ox, oy in plane[::-1]:
         sx, sy, dev = at_chip(ox, oy)
         c = 4 * sy + sx
         got = hva.at[2 * c + core]
         heard_all(got, r_hva.at[c])
-        rcopy(got, got, s_hva, r_sib, exp_dev(sib)).start()
+        rcopy(got, got, s_hva, r_sib.at[sy], exp_dev(sib)).start()
     c_wo.wait()
-    heard_all(hva.at[pl.ds(0, C // 2)], r_sib)
-
-    for b in range(C // G):
-        blk = mm(perm[...], hva[b * G : (b + 1) * G].reshape(N2, DV)).astype(BF16)
+    for off in (0, 1, 3, 2):
+        y = lax.rem(cy + off, 4)
+        heard_all(hva.at[pl.ds(0, 4)], r_sib.at[y])
+        blk = mm(perm[...], hva[pl.ds(8 * y, 8)].reshape(N2, DV)).astype(BF16)
         for h in range(H):
-            xmat[b * NR : (b + 1) * NR, h * DV : (h + 1) * DV] = blk[h * NR : (h + 1) * NR]
+            at = pl.ds(pl.multiple_of(y * NR, NR), NR)
+            xmat[at, h * DV : (h + 1) * DV] = blk[h * NR : (h + 1) * NR]
     proj = mm_nt(xmat[...], wo[...])
     resid = (res_ref[...].astype(F32) + proj).astype(BF16).astype(F32)
-    xall[0, 0] = (resid * gain_ref[...]).astype(BF16)
+    xall[1, 0] = (resid * gain_ref[...]).astype(BF16)
 
     def x_copy(off, n):
         ref = xall.at[n // 4, n % 4]
-        return rcopy(xall.at[0, 0], ref, s_x, r_x.at[n], dp_dev(at_dp(off)))
+        return rcopy(xall.at[1, 0], ref, s_x, r_x.at[n], dp_dev(at_dp(off)))
 
     def fwd(n):
         src, dst = xall.at[n // 4, n % 4], xsib.at[n // 4, n % 4]
         return rcopy(src, dst, s_fw, r_fwd[n // 4], exp_dev(sib))
 
-    for off in (-1, 1, -2, 4, -3, 3, 2):
+    for off in others:
         x_copy(off, BACK[off]).start()
-    fwd(0).start()
+    fwd(ME).start()
     sq = jnp.sum(resid * resid, axis=1, keepdims=True)
     sq_row = jnp.broadcast_to(sq, (GROUP, 128)).T[0:1]
     sq_s[...] = jnp.concatenate([sq_row] * (128 // GROUP), axis=1)
@@ -543,7 +547,7 @@
 
     heard_all(sq_r.at[pl.ds(0, C - 1)], r_sq)
     inv_s[...] = lax.rsqrt(jnp.sum(sq_r[...], axis=0) / D + EPS)
-    inv_r[0] = inv_s[...]
+    inv_r[ME] = inv_s[...]
 
     def inv_copy(off, n):
         return rcopy(inv_s, inv_r.at[n], s_inv, r_inv, dp_dev(at_dp(off)))
@@ -553,21 +557,21 @@
     get_x(1)
     partials(1)
     relay(0)
+    relay(1)
     second(0)
-    relay(1)
-    heard_all(inv_r.at[pl.ds(1, G - 1)], r_inv)
+    second(1)
+    heard_all(inv_r.at[pl.ds(0, G - 1)], r_inv)
     hidden(0)
-    second(1)
+    hidden(1)
     spread(0)
-    hidden(1)
+    spread(1)
     c_wout.wait()
     heard_all(wout.at[1], r_wout)
     down(0)
-    spread(1)
     give_back(0)
     down(1)
     give_back(1)
-    total = resid + zown[0, 0:GROUP, :]
+    total = resid + zown[1, 0:GROUP, :]
 
     w1.wait_send()
     w2.wait_send()
@@ -586,9 +590,9 @@
     sent_all(wv.at[pl.ds(0, 30), pl.ds(0, 2 * QR)], s_hid)
     sent_all(zsib_r, s_zsib)
 
-    heard_all(zr.at[pl.ds(1, G - 1)], r_z)
-    for n in range(1, G):
-        total = total + zr[n].astype(F32)
+    heard_all(zr.at[seven], r_z)
+    for off in others:
+        total = total + zr[POS[off]].astype(F32)
     out_ref[...] = total.astype(BF16)
     sent_all(zr.at[seven], s_z)
 
@@ -634,7 +638,7 @@
         v((2, 2, 4, QR, QC)), v((2, 4, SLOTS, QC // 2)), v((2, SLOTS, W)), v((2, SLOTS, W)),
         v((2, HALF, W)), v((2, HALF, W)), v((2, 4, GROUP, W)), v((G, GROUP, W)),
         v((2, HALF, W), F32),
-        dma(14), dma(16), dma(13), dma(G), dma(G), dma(C // 2), dma(12), dma(4), dma(18),
+        dma(14), dma(16), dma(12), dma(G), dma(G), dma(C // 2), dma(4), dma(12), dma(4), dma(18),
     ]
     vm = pl.BlockSpec(memory_space=pltpu.VMEM)
     hbm = pl.BlockSpec(memory_space=pl.ANY)

time: 86.7 us -> 83.2 us (0.960)
  Pallas kernels: 85.2 us -> 81.7 us
    pallas_call x1, Pallas kernels: 85.2 us -> 81.7 us  [body(): pl.pallas_call(functools.partial(kernel, G, C, ELOC, capacity), out_shape...]
where the time goes in v4:
time: 83.2 us; the launch traced here: 83 us
  Pallas kernels  81.7 us (98%)
  local copies, waits for them, and re-layouts  1.38 us (2%)
    pallas_call x1, Pallas kernels, body(): pl.pallas_call(functools.partial(kernel, G, C, ELOC, capacity), out_shape...  81.7 us

profile of v4, /device:TPU:1, one launch (start us, length us, event | category | flops | bytes accessed | tf_op | source)
XLA Modules:
  0.0 83.0 jit_solution(354750850587647459)
XLA Ops:
  0.0 81.7 %decode_step.1 = bf16[64,224]{1,0:T(8,128)(2,1)} custom-call(bf16[2,32,576]{2,1,0:T(8,128)(2,1)} %q_hbm.1, bf16[2,576]{1,0:T(2,128)(2,1)} %nl_hbm.1, bf16[6,576,128]{2,1,0:T(8,128)(2,1)} %pool_hbm.1, s32[8,1,2,8]{3,2,1,0:T(2,128)} %owner_hbm.1, s32[8,1,2,8]{3,2,1,0:T(2,128)} %slot_hbm.1, s32[2]{0:T(128)} %len_hbm.1, bf16[64,224]{1,0:T(8,128)(2,1)} %res_hbm.1, ...), custom_call_target="tpu_custom_call" | custom-call | flops 4294967296 | bytes 16777216 | tf_op jit(solution)/shard_map/decode_step/pallas_call | solution.py:645
  81.7 1.4 %copy.16 = bf16[64,224]{1,0:T(8,128)(2,1)} copy(bf16[64,224]{1,0:T(8,128)(2,1)} %decode_step.1) | data formatting | bytes 57344

commit v5 on v4

--- a/solution.py
+++ b/solution.py
@@ -42,8 +42,8 @@
     nl_ref, owner_ref, slot_ref, len_ref, res_ref, gain_ref, ids_ref, gates_ref,
     kc, vt, nlp, q_in, q_all, sml_s, sml_r, perm, perm_t, o_all, o_hm, hv_hm, hv_s, lse_s, hv_r,
     lse_r, hva, xmat, wv, wo, win, wg, wout, xall, xsib, sq_s, sq_r, inv_s, inv_r,
-    sel, sel_t, gcol, part, in1, out1, b2, in2, hid, vown, vsib, zsib_s, zsib_r, zs, zr, zown,
-    lsem, sent, heard, r_q, r_x, r_hva, r_sib, r_p1, r_p2, r_hid,
+    sel, sel_g, sel_t, gcol, part, in1, b2, in2, hid, vown, vsib, zsib_s, zsib_r, zs, zr, zown,
+    lsem, sent, heard, r_rows, r_q, r_x, r_p1, r_p2, r_hid,
 ):
     g = lax.axis_index("dp")
     k = lax.axis_index("expert")
@@ -83,7 +83,7 @@
 
     s_q, s_sml, s_hv, s_lse, s_hva, s_x, s_fw, s_sq = (sent.at[i] for i in range(8))
     s_inv, s_p1, s_p2, s_hid, s_win, s_wout, s_zsib, s_z = (sent.at[8 + i] for i in range(8))
-    r_sml, r_hv, r_lse, r_inv, r_z, r_sq, r_win, r_wout = (heard.at[i] for i in range(8))
+    r_sml, r_lse, r_inv, r_z, r_sq, r_win, r_wout = (heard.at[i] for i in range(7))
     r_fwd, r_zsib = (heard.at[8], heard.at[9]), (heard.at[10], heard.at[11])
 
     def rcopy(src, dst, ss, rs, dev):
@@ -187,6 +187,10 @@
     pr = iota((N2, 1), 0)
     perm[...] = (iota((N2, N2), 1) == lax.rem(pr, NR) * H + lax.div(pr, NR)).astype(BF16)
     perm_t[...] = (iota((N2, N2), 1) == lax.rem(pr, H) * NR + lax.div(pr, H)).astype(BF16)
+    rr = iota((GROUP, GROUP), 0)
+    rc = iota((GROUP, GROUP), 1)
+    to_split = (rc == lax.rem(rr, C) * ROWS + lax.div(rr, C)).astype(BF16)
+    from_split = (rr == lax.rem(rc, C) * ROWS + lax.div(rc, C)).astype(BF16)
     nl = nl_ref[...].astype(F32)
     nrow = iota((128, LAT), 0)
     nacc = jnp.zeros((128, LAT), F32)
@@ -310,33 +314,46 @@
     hv_r[g] = hv_s[g]
     lse_r[g] = lse_s[g]
 
-    def send_hv(d):
+    def part_of(r):
+        return pl.ds(r * H, H)
+
+    def send_hv(r, d):
         j = dp_peer(d)
-        rcopy(lse_s.at[j], lse_r.at[g], s_lse, r_lse, dp_dev(j)).start()
-        rcopy(hv_s.at[j], hv_r.at[g], s_hv, r_hv, dp_dev(j)).start()
-
-    loop(1, G, send_hv)
+        if r == 0:
+            rcopy(lse_s.at[j], lse_r.at[g], s_lse, r_lse, dp_dev(j)).start()
+        rcopy(
+            hv_s.at[j, part_of(r)], hv_r.at[g, part_of(r)], s_hv, r_rows.at[r], dp_dev(j)
+        ).start()
+
+    for r in range(ROWS):
+        loop(1, G, functools.partial(send_hv, r))
 
     heard_all(win.at[1], r_win)
     loop(0, ELOC, lambda e: split(1, e))
     heard_all(sml_r.at[pl.ds(0, G - 1)], r_sml)
     siota = iota((ESL, 4 * GROUP), 0).astype(F32)
+    codes_in = sml_r[:, :, 0:GROUP].reshape(8 * G, GROUP).astype(BF16)
+    split_codes = mm(codes_in, from_split)
+
+    def slots(rows, w, e):
+        return jnp.concatenate(
+            [jnp.where(c >= 0, c + float(t * CAPX), -1.0) for t, c in enumerate(rows)], axis=1
+        )
+
     for w in range(2):
         for e in range(ELOC):
-            codes = []
-            gvals = []
-            for t in range(4):
-                cj = sml_r[4 * w + t, e : e + 1, 0:GROUP]
-                codes.append(jnp.where(cj >= 0, cj + float(t * CAPX), -1.0))
-                gvals.append(sml_r[4 * w + t, ELOC + e : ELOC + e + 1, 0:GROUP])
-            hit = siota == jnp.concatenate(codes, axis=1)
-            sel[w, e] = hit.astype(F32).astype(BF16)
-            gs = jnp.where(hit, jnp.concatenate(gvals, axis=1), 0.0)
+            ns = [4 * w + t for t in range(4)]
+            given = siota == slots([sml_r[n, e : e + 1, 0:GROUP] for n in ns], w, e)
+            halved = siota == slots([split_codes[8 * n + e : 8 * n + e + 1] for n in ns], w, e)
+            sel[w, e] = halved.astype(F32).astype(BF16)
+            sel_g[w, e] = given.astype(F32).astype(BF16)
+            gvals = [sml_r[n, ELOC + e : ELOC + e + 1, 0:GROUP] for n in ns]
+            gs = jnp.where(given, jnp.concatenate(gvals, axis=1), 0.0)
             gcol[w, e] = jnp.broadcast_to(jnp.sum(gs, axis=1, keepdims=True), (ESL, 128))
-        sel_t[w] = sel[w].reshape(ELOC * ESL, 4 * GROUP).T
+        sel_t[w] = sel_g[w].reshape(ELOC * ESL, 4 * GROUP).T
+    res_split = mm(to_split, res_ref[...])
 
     heard_all(lse_r.at[pl.ds(0, G - 1)], r_lse)
-    heard_all(hv_r.at[pl.ds(0, G - 1)], r_hv)
     riota = iota((8, 128), 0)
     ls = jnp.full((8, 128), NEG, F32)
     for j in range(G):
@@ -344,45 +361,48 @@
     wts = jnp.exp(ls - jnp.max(ls, axis=0, keepdims=True))
     wts = wts / jnp.sum(wts, axis=0, keepdims=True)
     wcol = wts.T
-    comb = jnp.zeros((RH, DV), F32)
-    for j in range(G):
-        comb = comb + wcol[0:RH, j : j + 1] * hv_r[j].astype(F32)
-    hva[k] = comb.astype(BF16)
-
     plane = [(2, 2), (2, 1), (2, -1), (1, 2), (-1, 2), (2, 0), (0, 2)]
     plane += [(1, 1), (1, -1), (-1, 1), (-1, -1), (1, 0), (-1, 0), (0, 1), (0, -1)]
-    for ox, oy in plane:
-        rcopy(hva.at[k], hva.at[k], s_hva, r_hva.at[chip], at_chip(ox, oy)[2]).start()
-    rcopy(hva.at[k], hva.at[k], s_hva, r_sib.at[cy], exp_dev(sib)).start()
-    for ox, oy in plane[::-1]:
-        sx, sy, dev = at_chip(ox, oy)
-        c = 4 * sy + sx
-        got = hva.at[2 * c + core]
-        heard_all(got, r_hva.at[c])
-        rcopy(got, got, s_hva, r_sib.at[sy], exp_dev(sib)).start()
+
+    for r in range(ROWS):
+        heard_all(hv_r.at[pl.ds(0, G - 1), part_of(0)], r_rows.at[r])
+        comb = jnp.zeros((H, DV), F32)
+        for j in range(G):
+            at = slice(r * H, (r + 1) * H)
+            comb = comb + wcol[at, j : j + 1] * hv_r[j, at].astype(F32)
+        hva[r, k] = comb.astype(BF16)
+        for ox, oy in plane:
+            x, y, dev = at_chip(ox, oy)
+            for kk in (2 * (4 * y + x) + core, 2 * (4 * y + x) + 1 - core):
+                rcopy(hva.at[r, k], hva.at[r, k], s_hva, r_rows.at[ROWS + r], exp_dev(kk)).start()
+        rcopy(hva.at[r, k], hva.at[r, k], s_hva, r_rows.at[ROWS + r], exp_dev(sib)).start()
     c_wo.wait()
-    for off in (0, 1, 3, 2):
-        y = lax.rem(cy + off, 4)
-        heard_all(hva.at[pl.ds(0, 4)], r_sib.at[y])
-        blk = mm(perm[...], hva[pl.ds(8 * y, 8)].reshape(N2, DV)).astype(BF16)
-        for h in range(H):
-            at = pl.ds(pl.multiple_of(y * NR, NR), NR)
-            xmat[at, h * DV : (h + 1) * DV] = blk[h * NR : (h + 1) * NR]
-    proj = mm_nt(xmat[...], wo[...])
-    resid = (res_ref[...].astype(F32) + proj).astype(BF16).astype(F32)
-    xall[1, 0] = (resid * gain_ref[...]).astype(BF16)
-
-    def x_copy(off, n):
-        ref = xall.at[n // 4, n % 4]
-        return rcopy(xall.at[1, 0], ref, s_x, r_x.at[n], dp_dev(at_dp(off)))
+
+    def half(r):
+        return pl.ds(r * C, C)
+
+    def x_copy(off, n, r):
+        ref = xall.at[n // 4, n % 4, half(r)]
+        return rcopy(xall.at[1, 0, half(r)], ref, s_x, r_x.at[n], dp_dev(at_dp(off)))
 
     def fwd(n):
         src, dst = xall.at[n // 4, n % 4], xsib.at[n // 4, n % 4]
         return rcopy(src, dst, s_fw, r_fwd[n // 4], exp_dev(sib))
 
-    for off in others:
-        x_copy(off, BACK[off]).start()
+    resids = []
+    for r in range(ROWS):
+        heard_all(hva.at[r, pl.ds(0, C - 1)], r_rows.at[ROWS + r])
+        for b in range(C // NR):
+            blk = mm(perm[...], hva[r, b * NR : (b + 1) * NR].reshape(N2, DV)).astype(BF16)
+            for h in range(H):
+                xmat[r, b * NR : (b + 1) * NR, h * DV : (h + 1) * DV] = blk[h * NR : (h + 1) * NR]
+        proj = mm_nt(xmat[r], wo[...])
+        resids.append((res_split[r * C : (r + 1) * C] + proj).astype(BF16).astype(F32))
+        xall[1, 0, r * C : (r + 1) * C] = (resids[r] * gain_ref[...]).astype(BF16)
+        for off in others:
+            x_copy(off, BACK[off], r).start()
     fwd(ME).start()
+    resid = jnp.concatenate(resids, axis=0)
     sq = jnp.sum(resid * resid, axis=1, keepdims=True)
     sq_row = jnp.broadcast_to(sq, (GROUP, 128)).T[0:1]
     sq_s[...] = jnp.concatenate([sq_row] * (128 // GROUP), axis=1)
@@ -397,8 +417,9 @@
     def get_x(w):
         for off in sorted(WAVES[w], key=abs):
             if off != 0:
-                x_copy(off, POS[off]).wait_recv()
-                fwd(POS[off]).start()
+                n = POS[off]
+                heard_all(xall.at[n // 4, n % 4], r_x.at[n])
+                fwd(n).start()
         heard_all(xsib.at[w], r_fwd[w])
 
     place = (cx, cy)
@@ -409,9 +430,10 @@
     def across(h, off):
         return at_chip(0, off)[2] if h == 0 else at_chip(off, 0)[2]
 
-    def ring1(w, h, slot, src):
-        sem = r_p1.at[3 * (2 * w + h) + min(slot, 2)]
-        return rcopy(src, in1.at[w, h, slot], s_p1, sem, along(h, 1 if slot in (0, 2, 3) else -1))
+    def ring1(w, h, role, e):
+        ref = part.at[w, pl.ds(2 * h, 2), block(e)]
+        dst = in1.at[w, h, role - 1]
+        return rcopy(ref, dst, s_p1, r_p1.at[2 * w + h], along(h, role))
 
     def block(e):
         return pl.ds(pl.multiple_of(e * ESL, 16), ESL)
@@ -428,29 +450,11 @@
             for h in range(2):
                 role = lax.rem(e - place[h] + 4, 4)
 
-                @pl.when(role == 2)
+                @pl.when(role > 0)
                 def _():
-                    ring1(w, h, 0, part.at[w, 2 * h, block(e)]).start()
-                    ring1(w, h, 1, part.at[w, 2 * h + 1, block(e)]).start()
-
-                @pl.when(role == 1)
-                def _():
-                    ring1(w, h, 2, part.at[w, 2 * h + 1, block(e)]).start()
-
-                @pl.when(role == 3)
-                def _():
-                    ring1(w, h, 4, part.at[w, 2 * h, block(e)]).start()
+                    ring1(w, h, role, e).start()
 
         loop(0, 4, step)
-
-    def relay(w):
-        for h in range(2):
-            for i in range(2):
-                to = lax.rem(place[h] + (1, 3)[i], 4)
-                ring1(w, h, i, in1.at[w, h, i]).wait_recv()
-                passed = part[w, 2 * h + i, block(to)].astype(F32) + in1[w, h, i].astype(F32)
-                out1[w, h, i] = passed.astype(BF16)
-                ring1(w, h, 3 + 2 * i, out1.at[w, h, i]).start()
 
     def rows2(p):
         return pl.ds(pl.multiple_of(lax.div(p, 2) * QR, 16), QR)
@@ -462,11 +466,12 @@
 
     def second(w):
         for h in range(2):
-            heard_all(in1.at[w, h, pl.ds(2, 4)], r_p1.at[3 * (2 * w + h) + 2])
+            heard_all(in1.at[w, h], r_p1.at[2 * w + h])
             for i in range(2):
-                own = part[w, 2 * h + i, block(place[h])].astype(F32)
-                got = in1[w, h, 4 - 2 * i].astype(F32) + in1[w, h, 3 + 2 * i].astype(F32)
-                b2[w, h, i] = (own + got).astype(BF16)
+                tot = part[w, 2 * h + i, block(place[h])].astype(F32)
+                for j in range(3):
+                    tot = tot + in1[w, h, j, i].astype(F32)
+                b2[w, h, i] = tot.astype(BF16)
             for off in (2, 1, 3):
                 ring2(w, h, off).start()
             p = place[1 - h]
@@ -477,11 +482,9 @@
         at = p[h] * ESL + lax.div(p[1 - h], 2) * QR
         return w, 2 * h + lax.rem(p[1 - h], 2), pl.ds(pl.multiple_of(at, 16), QR)
 
-    around = [(1, 1), (1, -1), (-1, 1), (-1, -1), (1, 0), (-1, 0), (0, 1), (0, -1)]
-
-    def hid_copy(w, h, sx, sy, n, dev):
-        ref = hid.at[piece(w, h, sx, sy)]
-        return rcopy(ref, ref, s_hid, r_hid.at[9 * w + n], dev)
+    def hid_copy(w, h, dev):
+        ref = hid.at[piece(w, h, cx, cy)]
+        return rcopy(ref, ref, s_hid, r_hid.at[w], dev)
 
     def hidden(w):
         irow = jnp.concatenate([inv_r[4 * w + t, 0:1, 0:GROUP] for t in range(4)], axis=1)
@@ -496,23 +499,11 @@
             ga = tot[:, 0:QF]
             hv = ga / (1.0 + jnp.exp(-ga)) * tot[:, QF : 2 * QF]
             hid[piece(w, h, cx, cy)] = hv.astype(BF16)
-            for ox, oy in around:
-                n = around.index((-ox, -oy))
-                hid_copy(w, h, cx, cy, n, at_chip(ox, oy)[2]).start()
-
-    def spread(w):
-        for n, (ox, oy) in enumerate(around):
-            sx, sy, _ = at_chip(ox, oy)
-            heard_all(hid.at[w, pl.ds(0, 2), pl.ds(0, QR)], r_hid.at[9 * w + n])
-            if ox == oy:
-                hid_copy(w, int(ox > 0), sx, sy, 8, at_chip(-ox, -oy)[2]).start()
-            if ox != 0:
-                hid_copy(w, int(ox > 0), sx, sy, 8, at_chip(-ox, 0)[2]).start()
-            if oy != 0:
-                hid_copy(w, int(oy > 0), sx, sy, 8, at_chip(0, -oy)[2]).start()
+            for ox, oy in plane:
+                hid_copy(w, h, at_chip(ox, oy)[2]).start()
 
     def down(w):
-        heard_all(hid.at[w, pl.ds(0, 2), pl.ds(0, 7 * QR)], r_hid.at[9 * w + 8])
+        heard_all(wv.at[pl.ds(0, 30), pl.ds(0, QR)], r_hid.at[w])
 
         def step(e):
             at = block(e)
@@ -556,22 +547,18 @@
         inv_copy(off, BACK[off]).start()
     get_x(1)
     partials(1)
-    relay(0)
-    relay(1)
     second(0)
     second(1)
     heard_all(inv_r.at[pl.ds(0, G - 1)], r_inv)
     hidden(0)
     hidden(1)
-    spread(0)
-    spread(1)
     c_wout.wait()
     heard_all(wout.at[1], r_wout)
     down(0)
     give_back(0)
     down(1)
     give_back(1)
-    total = resid + zown[1, 0:GROUP, :]
+    total = mm(from_split, resid.astype(BF16)) + zown[1, 0:GROUP, :]
 
     w1.wait_send()
     w2.wait_send()
@@ -580,7 +567,7 @@
     sent_all(sml_r.at[seven], s_sml)
     sent_all(hv_r.at[seven], s_hv)
     sent_all(lse_r.at[seven], s_lse)
-    sent_all(hva.at[pl.ds(0, C - 1)], s_hva)
+    sent_all(hva.at[:, pl.ds(0, C - 1)], s_hva)
     sent_all(zr.at[seven], s_x)
     sent_all(zr, s_fw)
     sent_all(sq_r.at[pl.ds(0, C - 1)], s_sq)
@@ -629,16 +616,16 @@
         v((G, 8, 128), F32), v((G, 8, 128), F32), v((N2, N2)), v((N2, N2)),
         v((N2, KVR)), v((N2, KVR)), v((N2, DV)), v((G, RH, DV)), v((G, 1, 128), F32),
         v((G, RH, DV)), v((G, 1, 128), F32),
-        v((C, RH, DV)), v((GROUP, H * DV)), v((H, KVR, DV)), v((W, H * DV)),
+        v((ROWS, C, H, DV)), v((ROWS, C, H * DV)), v((H, KVR, DV)), v((W, H * DV)),
         v((2, ELOC, W, 2, FH)), v((ELOC, 2, W, FF)), v((2, ELOC, W, FH)),
         v((2, 4, GROUP, W)), v((2, 4, GROUP, W)), v((1, 128), F32), v((C, 1, 128), F32),
         v((1, 128), F32), v((G, 1, 128), F32),
-        v((2, ELOC, ESL, HALF)), v((2, HALF, SLOTS)), v((2, ELOC, ESL, 128), F32),
-        v((2, 4, SLOTS, QC)), v((2, 2, 6, ESL, QC)), v((2, 2, 2, ESL, QC)), v((2, 2, 2, ESL, QC)),
+        v((2, ELOC, ESL, HALF)), v((2, ELOC, ESL, HALF)), v((2, HALF, SLOTS)), v((2, ELOC, ESL, 128), F32),
+        v((2, 4, SLOTS, QC)), v((2, 2, 3, 2, ESL, QC)), v((2, 2, 2, ESL, QC)),
         v((2, 2, 4, QR, QC)), v((2, 4, SLOTS, QC // 2)), v((2, SLOTS, W)), v((2, SLOTS, W)),
         v((2, HALF, W)), v((2, HALF, W)), v((2, 4, GROUP, W)), v((G, GROUP, W)),
         v((2, HALF, W), F32),
-        dma(14), dma(16), dma(12), dma(G), dma(G), dma(C // 2), dma(4), dma(12), dma(4), dma(18),
+        dma(14), dma(16), dma(12), dma(2 * ROWS), dma(G), dma(G), dma(4), dma(4), dma(2),
     ]
     vm = pl.BlockSpec(memory_space=pltpu.VMEM)
     hbm = pl.BlockSpec(memory_space=pl.ANY)

time: 83.2 us -> 80.7 us (0.970)
  Pallas kernels: 81.7 us -> 79.2 us
    pallas_call x1, Pallas kernels: 81.7 us -> 79.2 us  [body(): pl.pallas_call(functools.partial(kernel, G, C, ELOC, capacity), out_shape...]
where the time goes in v5:
time: 80.7 us; the launch traced here: 80.6 us
  Pallas kernels  79.2 us (98%)
  local copies, waits for them, and re-layouts  1.38 us (2%)
    pallas_call x1, Pallas kernels, body(): pl.pallas_call(functools.partial(kernel, G, C, ELOC, capacity), out_shape...  79.2 us

profile of v5, /device:TPU:1, one launch (start us, length us, event | category | flops | bytes accessed | tf_op | source)
XLA Modules:
  0.0 80.6 jit_solution(12724252451533548910)
XLA Ops:
  0.0 79.2 %decode_step.1 = bf16[64,224]{1,0:T(8,128)(2,1)} custom-call(bf16[2,32,576]{2,1,0:T(8,128)(2,1)} %q_hbm.1, bf16[2,576]{1,0:T(2,128)(2,1)} %nl_hbm.1, bf16[6,576,128]{2,1,0:T(8,128)(2,1)} %pool_hbm.1, s32[8,1,2,8]{3,2,1,0:T(2,128)} %owner_hbm.1, s32[8,1,2,8]{3,2,1,0:T(2,128)} %slot_hbm.1, s32[2]{0:T(128)} %len_hbm.1, bf16[64,224]{1,0:T(8,128)(2,1)} %res_hbm.1, ...), custom_call_target="tpu_custom_call" | custom-call | flops 4294967296 | bytes 16777216 | tf_op jit(solution)/shard_map/decode_step/pallas_call | solution.py:632
  79.2 1.4 %copy.16 = bf16[64,224]{1,0:T(8,128)(2,1)} copy(bf16[64,224]{1,0:T(8,128)(2,1)} %decode_step.1) | data formatting | bytes 57344

commit v6 on v5

--- a/solution.py
+++ b/solution.py
@@ -41,8 +41,8 @@
     out_ref,
     nl_ref, owner_ref, slot_ref, len_ref, res_ref, gain_ref, ids_ref, gates_ref,
     kc, vt, nlp, q_in, q_all, sml_s, sml_r, perm, perm_t, o_all, o_hm, hv_hm, hv_s, lse_s, hv_r,
-    lse_r, hva, xmat, wv, wo, win, wg, wout, xall, xsib, sq_s, sq_r, inv_s, inv_r,
-    sel, sel_g, sel_t, gcol, part, in1, b2, in2, hid, vown, vsib, zsib_s, zsib_r, zs, zr, zown,
+    lse_r, hva, xmat, wv, wo, wot, win, wg, wout, woutt, xall, xsib, sq_s, sq_r, inv_s, inv_r,
+    sel, sel_g, sel_t, gcol, part, in1, out1, b2, in2, hid, vown, vsib, zsib_s, zsib_r, zs, zr, zown,
     lsem, sent, heard, r_rows, r_q, r_x, r_p1, r_p2, r_hid,
 ):
     g = lax.axis_index("dp")
@@ -266,6 +266,9 @@
     c_win.wait()
     loop(0, ELOC, lambda e: split(0, e))
 
+    c_wo.wait()
+    wot[...] = wo[...].T
+
     for i, off in ((0, -2), (1, 2)):
         src = at_dp(off)
         q_copy(src, off).wait_recv()
@@ -376,7 +379,6 @@
             for kk in (2 * (4 * y + x) + core, 2 * (4 * y + x) + 1 - core):
                 rcopy(hva.at[r, k], hva.at[r, k], s_hva, r_rows.at[ROWS + r], exp_dev(kk)).start()
         rcopy(hva.at[r, k], hva.at[r, k], s_hva, r_rows.at[ROWS + r], exp_dev(sib)).start()
-    c_wo.wait()
 
     def half(r):
         return pl.ds(r * C, C)
@@ -389,14 +391,23 @@
         src, dst = xall.at[n // 4, n % 4], xsib.at[n // 4, n % 4]
         return rcopy(src, dst, s_fw, r_fwd[n // 4], exp_dev(sib))
 
+    c_wout.wait()
+    heard_all(wout.at[1], r_wout)
+    for o in range(2):
+        for e in range(ELOC):
+            woutt[o, e] = wout[o, e].T
+
     resids = []
     for r in range(ROWS):
         heard_all(hva.at[r, pl.ds(0, C - 1)], r_rows.at[ROWS + r])
+        both = [hva[r, b * NR : (b + 1) * NR].reshape(N2, DV) for b in range(C // NR)]
+        blk = mm(perm[...], jnp.concatenate(both, axis=1)).astype(BF16)
         for b in range(C // NR):
-            blk = mm(perm[...], hva[r, b * NR : (b + 1) * NR].reshape(N2, DV)).astype(BF16)
             for h in range(H):
-                xmat[r, b * NR : (b + 1) * NR, h * DV : (h + 1) * DV] = blk[h * NR : (h + 1) * NR]
-        proj = mm_nt(xmat[r], wo[...])
+                xmat[r, b * NR : (b + 1) * NR, h * DV : (h + 1) * DV] = blk[
+                    h * NR : (h + 1) * NR, b * DV : (b + 1) * DV
+                ]
+        proj = mm(xmat[r], wot[...])
         resids.append((res_split[r * C : (r + 1) * C] + proj).astype(BF16).astype(F32))
         xall[1, 0, r * C : (r + 1) * C] = (resids[r] * gain_ref[...]).astype(BF16)
         for off in others:
@@ -430,10 +441,9 @@
     def across(h, off):
         return at_chip(0, off)[2] if h == 0 else at_chip(off, 0)[2]
 
-    def ring1(w, h, role, e):
-        ref = part.at[w, pl.ds(2 * h, 2), block(e)]
-        dst = in1.at[w, h, role - 1]
-        return rcopy(ref, dst, s_p1, r_p1.at[2 * w + h], along(h, role))
+    def ring1(w, h, slot, src):
+        sem = r_p1.at[3 * (2 * w + h) + min(slot, 2)]
+        return rcopy(src, in1.at[w, h, slot], s_p1, sem, along(h, 1 if slot in (0, 2, 3) else -1))
 
     def block(e):
         return pl.ds(pl.multiple_of(e * ESL, 16), ESL)
@@ -450,11 +460,29 @@
             for h in range(2):
                 role = lax.rem(e - place[h] + 4, 4)
 
-                @pl.when(role > 0)
+                @pl.when(role == 2)
                 def _():
-                    ring1(w, h, role, e).start()
+                    ring1(w, h, 0, part.at[w, 2 * h, block(e)]).start()
+                    ring1(w, h, 1, part.at[w, 2 * h + 1, block(e)]).start()
+
+                @pl.when(role == 1)
+                def _():
+                    ring1(w, h, 2, part.at[w, 2 * h + 1, block(e)]).start()
+
+                @pl.when(role == 3)
+                def _():
+                    ring1(w, h, 4, part.at[w, 2 * h, block(e)]).start()
 
         loop(0, 4, step)
+
+    def relay(w):
+        for h in range(2):
+            for i in range(2):
+                to = lax.rem(place[h] + (1, 3)[i], 4)
+                ring1(w, h, i, in1.at[w, h, i]).wait_recv()
+                passed = part[w, 2 * h + i, block(to)].astype(F32) + in1[w, h, i].astype(F32)
+                out1[w, h, i] = passed.astype(BF16)
+                ring1(w, h, 3 + 2 * i, out1.at[w, h, i]).start()
 
     def rows2(p):
         return pl.ds(pl.multiple_of(lax.div(p, 2) * QR, 16), QR)
@@ -466,12 +494,11 @@
 
     def second(w):
         for h in range(2):
-            heard_all(in1.at[w, h], r_p1.at[2 * w + h])
+            heard_all(in1.at[w, h, pl.ds(2, 4)], r_p1.at[3 * (2 * w + h) + 2])
             for i in range(2):
-                tot = part[w, 2 * h + i, block(place[h])].astype(F32)
-                for j in range(3):
-                    tot = tot + in1[w, h, j, i].astype(F32)
-                b2[w, h, i] = tot.astype(BF16)
+                own = part[w, 2 * h + i, block(place[h])].astype(F32)
+                got = in1[w, h, 4 - 2 * i].astype(F32) + in1[w, h, 3 + 2 * i].astype(F32)
+                b2[w, h, i] = (own + got).astype(BF16)
             for off in (2, 1, 3):
                 ring2(w, h, off).start()
             p = place[1 - h]
@@ -505,16 +532,16 @@
     def down(w):
         heard_all(wv.at[pl.ds(0, 30), pl.ds(0, QR)], r_hid.at[w])
 
-        def step(e):
-            at = block(e)
-            he = jnp.concatenate([hid[w, f, at] for f in range(4)], axis=1)
-            gs = gcol[w, e, :, 0:1]
-            vsib[w, at, :] = (mm_nt(he, wout[1, e]) * gs).astype(BF16)
-            vown[w, at, :] = (mm_nt(he, wout[0, e]) * gs).astype(BF16)
-
-        loop(0, ELOC, step)
+        def out(o, into):
+            for e in range(ELOC):
+                at = slice(e * ESL, (e + 1) * ESL)
+                he = jnp.concatenate([hid[w, f, at] for f in range(4)], axis=1)
+                into[w, at, :] = (mm(he, woutt[o, e]) * gcol[w, e, :, 0:1]).astype(BF16)
+
+        out(1, vsib)
         zsib_s[w] = mm(sel_t[w], vsib[w]).astype(BF16)
         zsib_copy(w).start()
+        out(0, vown)
         zown[w] = mm(sel_t[w], vown[w])
 
     def zsib_copy(w):
@@ -547,13 +574,13 @@
         inv_copy(off, BACK[off]).start()
     get_x(1)
     partials(1)
+    relay(0)
+    relay(1)
     second(0)
     second(1)
     heard_all(inv_r.at[pl.ds(0, G - 1)], r_inv)
     hidden(0)
     hidden(1)
-    c_wout.wait()
-    heard_all(wout.at[1], r_wout)
     down(0)
     give_back(0)
     down(1)
@@ -616,16 +643,16 @@
         v((G, 8, 128), F32), v((G, 8, 128), F32), v((N2, N2)), v((N2, N2)),
         v((N2, KVR)), v((N2, KVR)), v((N2, DV)), v((G, RH, DV)), v((G, 1, 128), F32),
         v((G, RH, DV)), v((G, 1, 128), F32),
-        v((ROWS, C, H, DV)), v((ROWS, C, H * DV)), v((H, KVR, DV)), v((W, H * DV)),
-        v((2, ELOC, W, 2, FH)), v((ELOC, 2, W, FF)), v((2, ELOC, W, FH)),
+        v((ROWS, C, H, DV)), v((ROWS, C, H * DV)), v((H, KVR, DV)), v((W, H * DV)), v((H * DV, W)),
+        v((2, ELOC, W, 2, FH)), v((ELOC, 2, W, FF)), v((2, ELOC, W, FH)), v((2, ELOC, FH, W)),
         v((2, 4, GROUP, W)), v((2, 4, GROUP, W)), v((1, 128), F32), v((C, 1, 128), F32),
         v((1, 128), F32), v((G, 1, 128), F32),
         v((2, ELOC, ESL, HALF)), v((2, ELOC, ESL, HALF)), v((2, HALF, SLOTS)), v((2, ELOC, ESL, 128), F32),
-        v((2, 4, SLOTS, QC)), v((2, 2, 3, 2, ESL, QC)), v((2, 2, 2, ESL, QC)),
+        v((2, 4, SLOTS, QC)), v((2, 2, 6, ESL, QC)), v((2, 2, 2, ESL, QC)), v((2, 2, 2, ESL, QC)),
         v((2, 2, 4, QR, QC)), v((2, 4, SLOTS, QC // 2)), v((2, SLOTS, W)), v((2, SLOTS, W)),
         v((2, HALF, W)), v((2, HALF, W)), v((2, 4, GROUP, W)), v((G, GROUP, W)),
         v((2, HALF, W), F32),
-        dma(14), dma(16), dma(12), dma(2 * ROWS), dma(G), dma(G), dma(4), dma(4), dma(2),
+        dma(14), dma(16), dma(12), dma(2 * ROWS), dma(G), dma(G), dma(12), dma(4), dma(2),
     ]
     vm = pl.BlockSpec(memory_space=pltpu.VMEM)
     hbm = pl.BlockSpec(memory_space=pl.ANY)

time: 80.7 us -> 79.7 us (0.988)
  Pallas kernels: 79.2 us -> 78.1 us
    pallas_call x1, Pallas kernels: 79.2 us -> 78.1 us  [body(): pl.pallas_call(functools.partial(kernel, G, C, ELOC, capacity), out_shape...]
where the time goes in v6:
time: 79.7 us; the launch traced here: 79.5 us
  Pallas kernels  78.1 us (98%)
  local copies, waits for them, and re-layouts  1.38 us (2%)
    pallas_call x1, Pallas kernels, body(): pl.pallas_call(functools.partial(kernel, G, C, ELOC, capacity), out_shape...  78.1 us

profile of v6, /device:TPU:1, one launch (start us, length us, event | category | flops | bytes accessed | tf_op | source)
XLA Modules:
  0.0 79.5 jit_solution(11672451422530752879)
XLA Ops:
  0.0 78.1 %decode_step.1 = bf16[64,224]{1,0:T(8,128)(2,1)} custom-call(bf16[2,32,576]{2,1,0:T(8,128)(2,1)} %q_hbm.1, bf16[2,576]{1,0:T(2,128)(2,1)} %nl_hbm.1, bf16[6,576,128]{2,1,0:T(8,128)(2,1)} %pool_hbm.1, s32[8,1,2,8]{3,2,1,0:T(2,128)} %owner_hbm.1, s32[8,1,2,8]{3,2,1,0:T(2,128)} %slot_hbm.1, s32[2]{0:T(128)} %len_hbm.1, bf16[64,224]{1,0:T(8,128)(2,1)} %res_hbm.1, ...), custom_call_target="tpu_custom_call" | custom-call | flops 4294967296 | bytes 16777216 | tf_op jit(solution)/shard_map/decode_step/pallas_call | solution.py:659
  78.1 1.4 %copy.16 = bf16[64,224]{1,0:T(8,128)(2,1)} copy(bf16[64,224]{1,0:T(8,128)(2,1)} %decode_step.1) | data formatting | bytes 57344

commit v7 on v6

--- a/solution.py
+++ b/solution.py
@@ -40,10 +40,10 @@
     ids_hbm, gates_hbm, win_hbm, wout_hbm,
     out_ref,
     nl_ref, owner_ref, slot_ref, len_ref, res_ref, gain_ref, ids_ref, gates_ref,
-    kc, vt, nlp, q_in, q_all, sml_s, sml_r, perm, perm_t, o_all, o_hm, hv_hm, hv_s, lse_s, hv_r,
+    kc, vt, nlp, q_in, q_main, q_rope, len_r, sml_s, sml_r, perm, perm_t, o_all, o_hm, hv_hm, hv_s, lse_s, hv_r,
     lse_r, hva, xmat, wv, wo, wot, win, wg, wout, woutt, xall, xsib, sq_s, sq_r, inv_s, inv_r,
     sel, sel_g, sel_t, gcol, part, in1, out1, b2, in2, hid, vown, vsib, zsib_s, zsib_r, zs, zr, zown,
-    lsem, sent, heard, r_rows, r_q, r_x, r_p1, r_p2, r_hid,
+    lsem, sent, heard, r_rows, r_q, r_rope, r_x, r_p1, r_p2, r_hid,
 ):
     g = lax.axis_index("dp")
     k = lax.axis_index("expert")
@@ -84,6 +84,7 @@
     s_q, s_sml, s_hv, s_lse, s_hva, s_x, s_fw, s_sq = (sent.at[i] for i in range(8))
     s_inv, s_p1, s_p2, s_hid, s_win, s_wout, s_zsib, s_z = (sent.at[8 + i] for i in range(8))
     r_sml, r_lse, r_inv, r_z, r_sq, r_win, r_wout = (heard.at[i] for i in range(7))
+    s_rope, s_len, r_len = sent.at[16], sent.at[17], heard.at[12]
     r_fwd, r_zsib = (heard.at[8], heard.at[9]), (heard.at[10], heard.at[11])
 
     def rcopy(src, dst, ss, rs, dev):
@@ -148,19 +149,36 @@
 
     c_q.wait()
     small[2].wait()
+    q_main[g] = q_in[:, :, 0:KVR]
+    q_rope[g] = jnp.concatenate([q_in[r, :, KVR:LAT] for r in range(ROWS)], axis=1)
+    lane = iota((1, 128), 1)
+    lens = jnp.zeros((1, 128), F32)
     for r in range(ROWS):
-        n = len_ref[r]
-        li = iota((H, q_all.shape[3] - LAT), 1)
-        tail = jnp.where(li == 0, lax.div(n, 32), jnp.where(li == 1, lax.rem(n, 32), 0))
-        q_all[g, r] = jnp.concatenate([q_in[r], tail.astype(F32).astype(BF16)], axis=1)
+        lens = jnp.where(lane == r, len_ref[r].astype(F32), lens)
+    len_r[g] = lens
     pl.semaphore_wait(barrier, G - 1 + C - 1)
 
-    def q_copy(src, off, row=None):
-        ref = q_all.at[src] if row is None else q_all.at[src, row]
+    def q_copy(src, off):
+        ref = q_main.at[src]
         return rcopy(ref, ref, s_q, r_q.at[src], dp_dev(at_dp(off)))
 
-    for off in (2, -2, 1, -1):
+    def rope_copy(src, off):
+        ref = q_rope.at[src]
+        return rcopy(ref, ref, s_rope, r_rope.at[src], dp_dev(at_dp(off)))
+
+    def len_copy(off):
+        ref = len_r.at[g]
+        return rcopy(ref, ref, s_len, r_len, dp_dev(at_dp(off)))
+
+    others = [4, -3, 3, -2, 2, -1, 1]
+    for off in others:
+        len_copy(off).start()
+    def send_q(off):
         q_copy(g, off).start()
+        rope_copy(g, off).start()
+
+    send_q(2)
+    send_q(-2)
 
     for i, c in enumerate(small):
         if i != 2:
@@ -211,16 +229,16 @@
     NT = NS * PAGE
 
     def attend(src, own):
-        qx = q_all[src].reshape(RH, q_all.shape[3])
-        q = qx[:, 0:LAT]
-        sc = mm(q, kc[...]) * scale
+        q = q_main[src].reshape(RH, KVR)
+        ropes = q_rope[src]
+        qr = jnp.concatenate([ropes[:, r * ROPE : (r + 1) * ROPE] for r in range(ROWS)], axis=0)
+        sc = (mm(q, kc[0:KVR, :]) + mm(qr, kc[KVR:LAT, :])) * scale
         lid = iota((1, NT), 1)
         slot_lane = lax.div(lid, PAGE)
         tpos = lax.rem(lid, PAGE).astype(F32)
         rows = []
         for s in range(ROWS):
-            lv = qx[s * H : s * H + 8, LAT : LAT + 2].astype(F32)
-            ln = lv[0:1, 0:1] * 32.0 + lv[0:1, 1:2]
+            ln = len_r[src][0:1, s : s + 1]
             cnt = jnp.zeros((1, NT), F32)
             for p in range(owner_ref.shape[3]):
                 here = jnp.where(owner_ref[src, 0, s, p] == g, slot_ref[src, 0, s, p], -1)
@@ -232,7 +250,8 @@
         top = jnp.max(scm, axis=1, keepdims=True)
         if own:
             cs = (iota((RH, 128), 1) == lax.div(iota((RH, 128), 0), H)).astype(F32)
-            ss = jnp.where(cs > 0, mm_nt(q, nlp[...]) * scale, NEG)
+            ss = (mm_nt(q, nlp[:, 0:KVR]) + mm_nt(qr, nlp[:, KVR:LAT])) * scale
+            ss = jnp.where(cs > 0, ss, NEG)
             top = jnp.maximum(top, jnp.max(ss, axis=1, keepdims=True))
         p = cnt * jnp.exp(scm - top)
         den = jnp.sum(p, axis=1, keepdims=True)
@@ -250,6 +269,9 @@
 
     attend(g, True)
 
+    send_q(1)
+    send_q(-1)
+
     col = iota((W, 2 * W), 1)
     two = 2 * iota((W, 2 * W), 0)
     pick_g = (col == two).astype(BF16)
@@ -271,15 +293,20 @@
 
     for i, off in ((0, -2), (1, 2)):
         src = at_dp(off)
-        q_copy(src, off).wait_recv()
+        heard_all(q_main.at[src], r_q.at[src])
+        heard_all(q_rope.at[src], r_rope.at[src])
         q_copy(src, 1 - 2 * i).start()
-        q_copy(src, 2 - 4 * i, row=i).start()
+        rope_copy(src, 1 - 2 * i).start()
+        row = q_main.at[src, i]
+        rcopy(row, row, s_q, r_q.at[src], dp_dev(at_dp(2 - 4 * i))).start()
+        if i == 0:
+            rope_copy(src, 2).start()
+    heard_all(len_r.at[pl.ds(0, G - 1)], r_len)
 
     def sml_copy(off, n):
         j = at_dp(off)
         return rcopy(sml_s.at[j], sml_r.at[n], s_sml, r_sml, dp_dev(j))
 
-    others = [4, -3, 3, -2, 2, -1, 1]
     for off in others:
         sml_copy(off, BACK[off]).start()
 
@@ -293,13 +320,15 @@
 
     def chunk(d):
         src = ring(d)
-        heard_all(q_all.at[src], r_q.at[src])
+        heard_all(q_main.at[src], r_q.at[src])
+        heard_all(q_rope.at[src], r_rope.at[src])
         attend(src, False)
 
     loop(0, 2, near)
     loop(2, G - 2, chunk)
     far = at_dp(G // 2)
-    heard_all(q_all.at[far], r_q.at[far])
+    heard_all(q_main.at[far], r_q.at[far])
+    heard_all(q_rope.at[far], r_rope.at[far])
     attend(far, False)
 
     o_hm[...] = mm(perm[...], o_all[...]).astype(BF16)
@@ -590,7 +619,9 @@
     w1.wait_send()
     w2.wait_send()
     seven = pl.ds(0, G - 1)
-    sent_all(q_all.at[seven], s_q)
+    sent_all(q_main.at[seven], s_q)
+    sent_all(q_rope.at[seven], s_rope)
+    sent_all(len_r.at[seven], s_len)
     sent_all(sml_r.at[seven], s_sml)
     sent_all(hv_r.at[seven], s_hv)
     sent_all(lse_r.at[seven], s_lse)
@@ -639,7 +670,7 @@
         pltpu.SMEM(page_slot.shape, jnp.int32), pltpu.SMEM(lengths.shape, jnp.int32),
         v((GROUP, W)), v((1, W), F32), v((TOP, GROUP), jnp.int32), v((TOP, GROUP), F32),
         v((LAT, NS * PAGE)), v((NS * PAGE, KVR)), v((128, LAT)), v((ROWS, H, LAT)),
-        v((G, ROWS, H, -(-(LAT + 2) // 128) * 128)),
+        v((G, ROWS, H, KVR)), v((G, H, ROWS * ROPE)), v((G, 1, 128), F32),
         v((G, 8, 128), F32), v((G, 8, 128), F32), v((N2, N2)), v((N2, N2)),
         v((N2, KVR)), v((N2, KVR)), v((N2, DV)), v((G, RH, DV)), v((G, 1, 128), F32),
         v((G, RH, DV)), v((G, 1, 128), F32),
@@ -652,7 +683,7 @@
         v((2, 2, 4, QR, QC)), v((2, 4, SLOTS, QC // 2)), v((2, SLOTS, W)), v((2, SLOTS, W)),
         v((2, HALF, W)), v((2, HALF, W)), v((2, 4, GROUP, W)), v((G, GROUP, W)),
         v((2, HALF, W), F32),
-        dma(14), dma(16), dma(12), dma(2 * ROWS), dma(G), dma(G), dma(12), dma(4), dma(2),
+        dma(14), dma(18), dma(13), dma(2 * ROWS), dma(G), dma(G), dma(G), dma(12), dma(4), dma(2),
     ]
     vm = pl.BlockSpec(memory_space=pltpu.VMEM)
     hbm = pl.BlockSpec(memory_space=pl.ANY)

time: 79.7 us -> 79.1 us (level)
  no operation moved by 1% of the time
where the time goes in v7:
time: 79.1 us; the launch traced here: 78.9 us
  Pallas kernels  77.5 us (98%)
  local copies, waits for them, and re-layouts  1.38 us (2%)
    pallas_call x1, Pallas kernels, body(): pl.pallas_call(functools.partial(kernel, G, C, ELOC, capacity), out_shape...  77.5 us

profile of v7, /device:TPU:1, one launch (start us, length us, event | category | flops | bytes accessed | tf_op | source)
XLA Modules:
  0.0 78.9 jit_solution(987917222079414952)
XLA Ops:
  0.0 77.5 %decode_step.1 = bf16[64,224]{1,0:T(8,128)(2,1)} custom-call(bf16[2,32,576]{2,1,0:T(8,128)(2,1)} %q_hbm.1, bf16[2,576]{1,0:T(2,128)(2,1)} %nl_hbm.1, bf16[6,576,128]{2,1,0:T(8,128)(2,1)} %pool_hbm.1, s32[8,1,2,8]{3,2,1,0:T(2,128)} %owner_hbm.1, s32[8,1,2,8]{3,2,1,0:T(2,128)} %slot_hbm.1, s32[2]{0:T(128)} %len_hbm.1, bf16[64,224]{1,0:T(8,128)(2,1)} %res_hbm.1, ...), custom_call_target="tpu_custom_call" | custom-call | flops 4294967296 | bytes 16777216 | tf_op jit(solution)/shard_map/decode_step/pallas_call | solution.py:690
  77.5 1.4 %copy.16 = bf16[64,224]{1,0:T(8,128)(2,1)} copy(bf16[64,224]{1,0:T(8,128)(2,1)} %decode_step.1) | data formatting | bytes 57344

commit v8 on v7

--- a/solution.py
+++ b/solution.py
@@ -144,8 +144,8 @@
     def sig_ex(d):
         pl.semaphore_signal(barrier, inc=1, device_id=exp_dev(ex_peer(d)), device_id_type=MESH)
 
+    loop(0, C - 1, lambda d: sig_ex(1 + lax.rem(d + C // 2 - 1, C - 1)))
     loop(1, G, sig_dp)
-    loop(1, C, sig_ex)
 
     c_q.wait()
     small[2].wait()
@@ -285,9 +285,6 @@
             wg[e, o, :, 2 * f * QF : (2 * f + 1) * QF] = wgate[:, f * QF : (f + 1) * QF]
             wg[e, o, :, (2 * f + 1) * QF : 2 * (f + 1) * QF] = wup[:, f * QF : (f + 1) * QF]
 
-    c_win.wait()
-    loop(0, ELOC, lambda e: split(0, e))
-
     c_wo.wait()
     wot[...] = wo[...].T
 
@@ -333,7 +330,7 @@
 
     o_hm[...] = mm(perm[...], o_all[...]).astype(BF16)
     c_wv.wait()
-    HB = 16
+    HB = 32
 
     def project(b):
         for i in range(HB):
@@ -419,6 +416,9 @@
     def fwd(n):
         src, dst = xall.at[n // 4, n % 4], xsib.at[n // 4, n % 4]
         return rcopy(src, dst, s_fw, r_fwd[n // 4], exp_dev(sib))
+
+    c_win.wait()
+    loop(0, ELOC, lambda e: split(0, e))
 
     c_wout.wait()
     heard_all(wout.at[1], r_wout)

time: 79.1 us -> 79.5 us (level)
  no operation moved by 1% of the time
where the time goes in v8:
time: 79.5 us; the launch traced here: 79.4 us
  Pallas kernels  78 us (98%)
  local copies, waits for them, and re-layouts  1.38 us (2%)
    pallas_call x1, Pallas kernels, body(): pl.pallas_call(functools.partial(kernel, G, C, ELOC, capacity), out_shape...  78 us

profile of v8, /device:TPU:1, one launch (start us, length us, event | category | flops | bytes accessed | tf_op | source)
XLA Modules:
  0.0 79.4 jit_solution(3419147586059724388)
XLA Ops:
  0.0 78.0 %decode_step.1 = bf16[64,224]{1,0:T(8,128)(2,1)} custom-call(bf16[2,32,576]{2,1,0:T(8,128)(2,1)} %q_hbm.1, bf16[2,576]{1,0:T(2,128)(2,1)} %nl_hbm.1, bf16[6,576,128]{2,1,0:T(8,128)(2,1)} %pool_hbm.1, s32[8,1,2,8]{3,2,1,0:T(2,128)} %owner_hbm.1, s32[8,1,2,8]{3,2,1,0:T(2,128)} %slot_hbm.1, s32[2]{0:T(128)} %len_hbm.1, bf16[64,224]{1,0:T(8,128)(2,1)} %res_hbm.1, ...), custom_call_target="tpu_custom_call" | custom-call | flops 4294967296 | bytes 16777216 | tf_op jit(solution)/shard_map/decode_step/pallas_call | solution.py:690
  78.0 1.4 %copy.16 = bf16[64,224]{1,0:T(8,128)(2,1)} copy(bf16[64,224]{1,0:T(8,128)(2,1)} %decode_step.1) | data formatting | bytes 57344
